TPU v7x, 128 devices: a whole 4x4x4 slice. The times are simulated.
128 devices in a mesh: seq: 16 (over z_lo, y, core), exp: 8 (over z_hi, x).
Axes of the slice: x: 4, y: 4, z: 4 (z_hi: 2, z_lo: 2; z = z_hi * 2 + z_lo), core: 2. Of those that a mesh axis runs over, the one named last changes fastest.
Arguments:
- resid: bfloat16 [16384, 2560], P(('seq', 'exp')), may hold values from -30 to 30
- queries: bfloat16 [16384, 1536], P('seq', 'exp'), may hold values from -6 to 6
- keyvals: bfloat16 [16384, 1024], P('seq', 'exp'), may hold values from -6 to 6
- out_proj: bfloat16 [1536, 2560], replicated, may hold values from -0.15625 to 0.15625
- norm_gain: bfloat16 [2560], replicated, may hold values from 0.099609375 to 1.8984375
- token_ids: int32 [16384], P(('seq', 'exp')), may hold values from 0 to 128255
- hash_table: int32 [128256], replicated, may hold values from 0 to 7
- w_gate: bfloat16 [8, 1024, 2560], P('exp', 'seq'), may hold values from -0.125 to 0.125
- w_up: bfloat16 [8, 1024, 2560], P('exp', 'seq'), may hold values from -0.125 to 0.125
- w_down: bfloat16 [8, 1024, 2560], P('exp', 'seq'), may hold values from -0.1875 to 0.1875
- cotangent: bfloat16 [16384, 2560], P(('seq', 'exp')), may hold values from -0.5 to 0.5
Outputs:
- layer_out: bfloat16 [16384, 2560], P(('seq', 'exp'))
- grad_gate: bfloat16 [8, 1024, 2560], P('exp', 'seq')
- grad_up: bfloat16 [8, 1024, 2560], P('exp', 'seq')
- grad_down: bfloat16 [8, 1024, 2560], P('exp', 'seq')
All inputs are finite; a program needn't handle non-finite values.
Results may differ from a plain program's by a relative error of at most 0.03.
Values may be sent and summed in bfloat16 or wider, within the bound.
A program may use at most 128 MiB of HBM per device.

v0:
```python
import math

import jax
import jax.numpy as jnp
from jax import lax
from jax.sharding import PartitionSpec as P

HEAD_DIM = 64


very_negative = -1e30
norm_eps = 1e-05
key_block_limit = 512


def fetch_weights(w_gate, w_up, w_down):
    return (
        lax.all_gather(w_gate, "seq", axis=1, tiled=True),
        lax.all_gather(w_up, "seq", axis=1, tiled=True),
        lax.all_gather(w_down, "seq", axis=1, tiled=True),
    )


def contract_rows(first_operand, second_operand):
    return lax.dot_general(
        first_operand, second_operand, (((0,), (0,)), ((), ())), preferred_element_type=jnp.float32
    )


def contract_cols(first_operand, second_operand):
    return lax.dot_general(
        first_operand, second_operand, (((1,), (1,)), ((), ())), preferred_element_type=jnp.float32
    )


def swiglu_forward(gate_act, up_act):
    sigmoid_gate = jax.nn.sigmoid(gate_act)
    silu_gate = gate_act * sigmoid_gate
    return (silu_gate * up_act).astype(jnp.bfloat16)


def swiglu_backward(gate_act, up_act, hidden_grad):
    sigmoid_gate = jax.nn.sigmoid(gate_act)
    silu_gate = gate_act * sigmoid_gate
    gate_grad = (
        hidden_grad * up_act * sigmoid_gate * (1.0 + gate_act * (1.0 - sigmoid_gate))
    ).astype(jnp.bfloat16)
    up_grad = (hidden_grad * silu_gate).astype(jnp.bfloat16)
    return (gate_grad, up_grad)


def attend(queries, keyvals):
    row_count = queries.shape[0]
    paired_heads = keyvals.shape[1] // (2 * HEAD_DIM)
    query_group_width = queries.shape[1] // (HEAD_DIM * paired_heads)
    score_scale = 1.0 / math.sqrt(HEAD_DIM)
    query_split = queries.reshape(row_count, paired_heads, query_group_width, HEAD_DIM)
    shard_first = lax.axis_index("seq") * row_count
    query_place = shard_first + jnp.arange(row_count, dtype=jnp.int32)
    last_query = shard_first + row_count - 1

    def compute(key_block, first_key, running):
        running_max, weight_sum, accumulated = running
        block_rows = key_block.shape[0]
        key_rows = key_block[:, :, 0, :]
        value_rows = key_block[:, :, 1, :]
        scores = (
            jnp.einsum("qkgd,nkd->kgqn", query_split, key_rows, preferred_element_type=jnp.float32)
            * score_scale
        )
        allowed = (first_key + jnp.arange(block_rows, dtype=jnp.int32))[None, :] <= query_place[
            :, None
        ]
        masked = jnp.where(allowed, scores, very_negative)
        new_max = jnp.maximum(running_max, jnp.max(masked, axis=3))
        weights = jnp.where(allowed, jnp.exp(masked - new_max[..., None]), 0.0)
        factor = jnp.exp(running_max - new_max)
        weight_sum = weight_sum * factor + jnp.sum(weights, axis=3)
        update = jnp.einsum(
            "kgqn,nkd->qkgd",
            weights.astype(jnp.bfloat16),
            value_rows,
            preferred_element_type=jnp.float32,
        )
        accumulated = accumulated * jnp.transpose(factor, (2, 0, 1))[..., None] + update
        return (new_max, weight_sum, accumulated)

    initial = (
        jnp.full((paired_heads, query_group_width, row_count), very_negative, jnp.float32),
        jnp.zeros((paired_heads, query_group_width, row_count), jnp.float32),
        jnp.zeros((row_count, paired_heads, query_group_width, HEAD_DIM), jnp.float32),
    )
    shard_rows = lax.all_gather(keyvals, "seq", axis=0, tiled=True)
    piece_rows = shard_rows.shape[0]
    block_rows = math.gcd(piece_rows, key_block_limit)
    pair_split = shard_rows.reshape(piece_rows, paired_heads, 2, HEAD_DIM)

    def one_block(block_index, current):
        first_key = block_index * block_rows
        key_block = lax.dynamic_slice_in_dim(pair_split, block_index * block_rows, block_rows, 0)
        return lax.cond(
            first_key > last_query,
            lambda kept: kept,
            lambda kept: compute(key_block, first_key, kept),
            current,
        )

    running_max, weight_sum, accumulated = lax.fori_loop(
        0, piece_rows // block_rows, one_block, initial
    )
    mixed_rows = accumulated / jnp.transpose(weight_sum, (2, 0, 1))[..., None]
    return mixed_rows.reshape(row_count, paired_heads * query_group_width * HEAD_DIM).astype(
        jnp.bfloat16
    )


def local(
    resid,
    queries,
    keyvals,
    out_proj,
    norm_gain,
    token_ids,
    hash_table,
    w_gate,
    w_up,
    w_down,
    cotangent,
):
    attention = attend(queries, keyvals)
    token_heads = lax.all_to_all(attention, "exp", split_axis=0, concat_axis=1, tiled=True)
    projected = jnp.dot(token_heads, out_proj, preferred_element_type=jnp.float32)
    hidden_state = (resid.astype(jnp.float32) + projected).astype(jnp.bfloat16)
    widened = hidden_state.astype(jnp.float32)
    mean_square = jnp.mean(widened * widened, axis=1, keepdims=True)
    normed = (widened * lax.rsqrt(mean_square + norm_eps) * norm_gain.astype(jnp.float32)).astype(
        jnp.bfloat16
    )
    token_count = resid.shape[0]
    model_width = resid.shape[1]
    expert_count = lax.axis_size("exp")
    capacity = token_count // expert_count
    expert_of = jnp.take(hash_table, token_ids)
    onehot_slots = (
        expert_of[:, None] == jnp.arange(expert_count, dtype=jnp.int32)[None, :]
    ).astype(jnp.int32)
    earlier = jnp.cumsum(onehot_slots, axis=0) - onehot_slots
    slot_of = jnp.sum(onehot_slots * earlier, axis=1)
    target = jnp.where(slot_of < capacity, expert_of * capacity + slot_of, -1)
    dispatch_table = (
        jnp.arange(expert_count * capacity, dtype=jnp.int32)[:, None] == target[None, :]
    ).astype(jnp.bfloat16)
    send_rows = (
        jnp.dot(dispatch_table, normed, preferred_element_type=jnp.float32)
        .astype(jnp.bfloat16)
        .reshape(expert_count, capacity, model_width)
    )
    send_grads = (
        jnp.dot(dispatch_table, cotangent, preferred_element_type=jnp.float32)
        .astype(jnp.bfloat16)
        .reshape(expert_count, capacity, model_width)
    )
    routed, routed_grads = (
        lax.all_to_all(send_rows, "exp", split_axis=0, concat_axis=0, tiled=True),
        lax.all_to_all(send_grads, "exp", split_axis=0, concat_axis=0, tiled=True),
    )
    expert_rows = routed.reshape(expert_count * capacity, model_width)
    output_grads = routed_grads.reshape(expert_count * capacity, model_width)
    full_gate, full_up, full_down = fetch_weights(w_gate, w_up, w_down)
    gate_act = contract_cols(expert_rows, full_gate[0])
    up_act = contract_cols(expert_rows, full_up[0])
    hidden_units = swiglu_forward(gate_act, up_act)
    expert_out = jnp.dot(hidden_units, full_down[0], preferred_element_type=jnp.float32).astype(
        jnp.bfloat16
    )
    hidden_grad = contract_cols(output_grads, full_down[0])
    gate_grad, up_grad = swiglu_backward(gate_act, up_act, hidden_grad)
    partial_gate = contract_rows(gate_grad, expert_rows)
    partial_up = contract_rows(up_grad, expert_rows)
    partial_down = contract_rows(hidden_units, output_grads)
    summed_gate, summed_up, summed_down = (
        lax.psum_scatter(
            partial_gate[None].astype(jnp.bfloat16), "seq", scatter_dimension=1, tiled=True
        ).astype(jnp.float32),
        lax.psum_scatter(
            partial_up[None].astype(jnp.bfloat16), "seq", scatter_dimension=1, tiled=True
        ).astype(jnp.float32),
        lax.psum_scatter(
            partial_down[None].astype(jnp.bfloat16), "seq", scatter_dimension=1, tiled=True
        ).astype(jnp.float32),
    )
    grad_gate = summed_gate.astype(jnp.bfloat16)
    grad_up = summed_up.astype(jnp.bfloat16)
    grad_down = summed_down.astype(jnp.bfloat16)
    returned_rows = lax.all_to_all(
        expert_out.reshape(expert_count, capacity, model_width),
        "exp",
        split_axis=0,
        concat_axis=0,
        tiled=True,
    )
    combined_output = contract_rows(
        dispatch_table, returned_rows.reshape(expert_count * capacity, model_width)
    )
    layer_out = (widened + combined_output).astype(jnp.bfloat16)
    return (layer_out, grad_gate, grad_up, grad_down)


def solution(mesh):
    in_specs = (
        P(("seq", "exp"), None),
        P("seq", "exp"),
        P("seq", "exp"),
        P(),
        P(),
        P(("seq", "exp")),
        P(),
        P("exp", "seq", None),
        P("exp", "seq", None),
        P("exp", "seq", None),
        P(("seq", "exp"), None),
    )
    out_specs = (
        P(("seq", "exp"), None),
        P("exp", "seq", None),
        P("exp", "seq", None),
        P("exp", "seq", None),
    )
    return jax.shard_map(local, mesh=mesh, in_specs=in_specs, out_specs=out_specs, check_vma=False)
```

profile of v0, /device:TPU:1, one launch (start us, length us, event | category | flops | bytes accessed | tf_op | source)
XLA Modules:
  0.0 708.0 jit_solution(16524123189469142138)
XLA Ops:
  7.2 0.7 all-gather.5.cloned.1.call-update
  8.0 0.7 all-gather.7.cloned.1.call-update
  8.7 0.7 all-gather.9.cloned.1.call-update
  9.5 0.5 all-gather.11.cloned.1.call-update
  10.0 0.7 compare_select_fusion
  10.7 2.0 gather_fusion
  12.6 0.7 and_select_fusion
  13.3 37.5 %all-gather.5.cloned.1.call-done = bf16[16384,128]{1,0:T(8,128)(2,1)} async-done(((bf16[1024,128]{1,0:T(8,128)(2,1)}), bf16[16384,128]{1,0:T(8,128)(2,1)}) %all-gather.5.cloned.1.call-update) | async-done | bytes 4194320 | tf_op jit(solution)/shard_map/all_gather | solution.py:93
  50.8 6.4 copy.23
  57.2 0.1 broadcast_in_dim.55
  57.3 50.6 %while.18 = (s32[]{:T(128)}, f32[1,3,1024]{2,1,0:T(4,128)S(1)}, f32[1,3,1024]{2,1,0:T(4,128)S(1)}, f32[1024,1,3,64]{0,3,2,1:T(8,128)S(1)}, s32[]{:T(128)}, /*ind...) while((s32[]{:T(128)}, f32[1,3,1024]{2,1,0:T(4,128)S(1)}, ...), condition=%wide.region_5.6_spmd.clone, body=%wide.region_0.5_spmd.clone.sunk | while | flops 424028672 | bytes 48451920 | solution.py:108
  57.3 12.0 %conditional.3 = (f32[1,3,1024]{2,1,0:T(4,128)S(1)}, f32[1,3,1024]{2,1,0:T(4,128)S(1)}, f32[1024,1,3,64]{0,3,2,1:T(8,128)S(1)}) conditional(s32[]{:T(128)} %convert_element_type.143, (s32[]{:T(128)}, s32[]{:T(128)}, bf16[16384,1,2,64]{0,3,2,1:T(8,128)(2,1)}, bf16[1024,1,3,64]{0,3,2,1:T(8,128)(2,1)S(1)}, f32[1,3,1024]{2,1,0:T(4,128)S(1)}, ...), branch_computations={%region_1.3_spmd, %region_4.4_spmd} | conditional | flops 424028672 | bytes 48423028 | solution.py:101
  57.4 0.4 broadcast_compare_fusion
  57.7 2.2 fusion.2
  60.0 2.6 copy-done.1
  62.6 1.6 fusion.4
  64.2 5.0 fusion.12
  69.3 12.0 %conditional.3 = (f32[1,3,1024]{2,1,0:T(4,128)S(1)}, f32[1,3,1024]{2,1,0:T(4,128)S(1)}, f32[1024,1,3,64]{0,3,2,1:T(8,128)S(1)}) conditional(s32[]{:T(128)} %convert_element_type.143, (s32[]{:T(128)}, s32[]{:T(128)}, bf16[16384,1,2,64]{0,3,2,1:T(8,128)(2,1)}, bf16[1024,1,3,64]{0,3,2,1:T(8,128)(2,1)S(1)}, f32[1,3,1024]{2,1,0:T(4,128)S(1)}, ...), branch_computations={%region_1.3_spmd, %region_4.4_spmd} | conditional | flops 424028672 | bytes 48423028 | solution.py:101
  69.4 0.4 broadcast_compare_fusion
  69.7 2.2 fusion.2
  72.0 2.6 copy-done.1
  74.6 1.6 fusion.4
  76.2 5.0 fusion.12
  81.4 11.9 %conditional.3 = (f32[1,3,1024]{2,1,0:T(4,128)S(1)}, f32[1,3,1024]{2,1,0:T(4,128)S(1)}, f32[1024,1,3,64]{0,3,2,1:T(8,128)S(1)}) conditional(s32[]{:T(128)} %convert_element_type.143, (s32[]{:T(128)}, s32[]{:T(128)}, bf16[16384,1,2,64]{0,3,2,1:T(8,128)(2,1)}, bf16[1024,1,3,64]{0,3,2,1:T(8,128)(2,1)S(1)}, f32[1,3,1024]{2,1,0:T(4,128)S(1)}, ...), branch_computations={%region_1.3_spmd, %region_4.4_spmd} | conditional | flops 424028672 | bytes 48423028 | solution.py:101
  81.4 0.4 broadcast_compare_fusion
  81.8 2.2 fusion.2
  84.0 2.6 copy-done.1
  86.6 1.6 fusion.4
  88.3 5.0 fusion.12
  93.3 12.1 %conditional.3 = (f32[1,3,1024]{2,1,0:T(4,128)S(1)}, f32[1,3,1024]{2,1,0:T(4,128)S(1)}, f32[1024,1,3,64]{0,3,2,1:T(8,128)S(1)}) conditional(s32[]{:T(128)} %convert_element_type.143, (s32[]{:T(128)}, s32[]{:T(128)}, bf16[16384,1,2,64]{0,3,2,1:T(8,128)(2,1)}, bf16[1024,1,3,64]{0,3,2,1:T(8,128)(2,1)S(1)}, f32[1,3,1024]{2,1,0:T(4,128)S(1)}, ...), branch_computations={%region_1.3_spmd, %region_4.4_spmd} | conditional | flops 424028672 | bytes 48423028 | solution.py:101
  93.3 0.4 broadcast_compare_fusion
  93.7 2.2 fusion.2
  95.9 2.6 copy-done.1
  98.6 1.6 fusion.4
  100.2 5.1 fusion.12
  107.9 0.1 divide_convert_fusion
  107.9 0.1 copy.26
  108.0 0.8 copy.24
  108.8 6.1 all-to-all-start
  114.9 0.1 fusion.45
  115.0 0.2 reduce_window_sum.11
  115.2 0.2 select_reduce_fusion
  115.4 8.3 %all-to-all-done = bf16[8,128,192]{1,2,0:T(8,128)(2,1)S(1)} async-done(((bf16[8,128,192]{1,2,0:T(8,128)(2,1)}), bf16[8,128,192]{1,2,0:T(8,128)(2,1)S(1)}, u32[]{:S(2)}, u32[]{:S(2)}) %all-to-all-start) | async-done | bytes 393248 | tf_op jit(solution)/shard_map/all_to_all | solution.py:131
  123.7 4.6 multiply_reduce_fusion
  128.3 1.2 convolution_convert_fusion.4
  129.6 3.5 all-to-all-start.1
  133.1 1.2 convolution_convert_fusion.3
  134.3 8.6 %all-to-all-done.1 = bf16[8,16,2560]{2,1,0:T(8,128)(2,1)S(1)} async-done(((bf16[8,16,2560]{2,1,0:T(8,128)(2,1)}), bf16[8,16,2560]{2,1,0:T(8,128)(2,1)S(1)}, u32[]{:S(2)}, u32[]{:S(2)}) %all-to-all-start.1) | async-done | bytes 655392 | tf_op jit(solution)/shard_map/all_to_all | solution.py:164
  142.9 4.2 all-to-all-start.3
  147.1 0.2 reduce-scatter.4.cloned.1.call-start
  147.4 4.3 fusion.29
  151.7 5.3 multiply_convert_fusion.4
  157.0 26.1 %all-gather.11.cloned.1.call-done = bf16[1,1024,2560]{2,1,0:T(8,128)(2,1)} async-done(((bf16[1,64,2560]{2,1,0:T(8,128)(2,1)}), bf16[1,1024,2560]{2,1,0:T(8,128)(2,1)}) %all-gather.11.cloned.1.call-update) | async-done | bytes 5242896 | tf_op jit(solution)/shard_map/all_gather | solution.py:20
  183.1 4.5 fusion.23
  187.7 3.9 fusion.31
  191.7 5.0 fusion.32
  196.7 0.0 reduce-scatter.8.cloned.1.call-start
  196.7 4.9 fusion.33
  201.7 3.3 fusion.37
  205.0 18.9 %all_to_all.31 = bf16[8,16,2560]{2,1,0:T(8,128)(2,1)S(1)} all-to-all(bf16[8,16,2560]{2,1,0:T(8,128)(2,1)S(1)} %bitcast.121), channel_id=1, replica_groups=mesh['seq'=16,'exp'=8] {'exp'}, dimensions={0} | all-to-all | bytes 1310720 | tf_op jit(solution)/shard_map/all_to_all | solution.py:195
  223.9 1.2 fusion.36
  225.1 334.5 %reduce-scatter.4.cloned.1.call-done = bf16[1,64,2560]{2,1,0:T(8,128)(2,1)} async-done(((bf16[1,1024,2560]{2,1,0:T(8,128)(2,1)}), bf16[1,64,2560]{2,1,0:T(8,128)(2,1)}) %reduce-scatter.4.cloned.1.call-update) | async-done | bytes 327696 | tf_op jit(solution)/shard_map/reduce_scatter | solution.py:182
  559.6 71.0 %reduce-scatter.6.cloned.1.call-done = bf16[1,64,2560]{2,1,0:T(8,128)(2,1)} async-done(((bf16[1,1024,2560]{2,1,0:T(8,128)(2,1)}), bf16[1,64,2560]{2,1,0:T(8,128)(2,1)}) %reduce-scatter.6.cloned.1.call-update) | async-done | bytes 327696 | tf_op jit(solution)/shard_map/reduce_scatter | solution.py:185
  630.6 70.5 %reduce-scatter.8.cloned.1.call-done = bf16[1,64,2560]{2,1,0:T(8,128)(2,1)} async-done(((bf16[1,1024,2560]{2,1,0:T(8,128)(2,1)}), bf16[1,64,2560]{2,1,0:T(8,128)(2,1)}) %reduce-scatter.8.cloned.1.call-update) | async-done | bytes 327696 | tf_op jit(solution)/shard_map/reduce_scatter | solution.py:188
  (171 shorter events, 1.9 us)
Async XLA Ops:
  7.2 125.9 %copy-start = (bf16[128,2560]{1,0:T(8,128)(2,1)S(1)}, bf16[128,2560]{1,0:T(8,128)(2,1)}, u32[]{:S(2)}) copy-start(bf16[128,2560]{1,0:T(8,128)(2,1)} %param.25) | copy-start | bytes 1966084
  7.2 43.6 %all-gather.5.cloned.1.call-start = ((), (), s32[]{:S(2)}) async-start(), calls=%async_computation.7 | async-start | bytes 4456448 | tf_op jit(solution)/shard_map/all_gather | solution.py:93
  7.9 139.4 %all-gather.7.cloned.1.call-start = ((), (), s32[]{:S(2)}) async-start(), calls=%async_computation.8 | async-start | bytes 5570560 | tf_op jit(solution)/shard_map/all_gather | solution.py:18
  8.7 48.6 %copy-start.4 = (bf16[1024,192]{0,1:T(8,128)(2,1)S(1)}, bf16[1024,192]{0,1:T(8,128)(2,1)}, u32[]{:S(2)}) copy-start(bf16[1024,192]{0,1:T(8,128)(2,1)} %param.16) | copy-start | bytes 1179652
  8.7 143.0 %all-gather.9.cloned.1.call-start = ((), (), s32[]{:S(2)}) async-start(), calls=%async_computation.9 | async-start | bytes 5570560 | tf_op jit(solution)/shard_map/all_gather | solution.py:19
  9.4 173.7 %all-gather.11.cloned.1.call-start = ((), (), s32[]{:S(2)}) async-start(), calls=%async_computation.10 | async-start | bytes 5570560 | tf_op jit(solution)/shard_map/all_gather | solution.py:20
  57.3 57.7 %copy-start.7 = (bf16[2560]{0:T(1024)(128)(2,1)S(1)}, bf16[2560]{0:T(1024)(128)(2,1)}, u32[]{:S(2)}) copy-start(bf16[2560]{0:T(1024)(128)(2,1)} %param.19) | copy-start | bytes 15364
  57.3 66.4 %copy-start.6 = (bf16[128,2560]{1,0:T(8,128)(2,1)S(1)}, bf16[128,2560]{1,0:T(8,128)(2,1)}, u32[]{:S(2)}) copy-start(bf16[128,2560]{1,0:T(8,128)(2,1)} %param.15) | copy-start | bytes 1966084
  59.9 2.7 copy-start.1
  72.0 2.7 copy-start.1
  84.0 2.7 copy-start.1
  95.9 2.7 copy-start.1
  108.8 14.9 %all-to-all-start = ((bf16[8,128,192]{1,2,0:T(8,128)(2,1)}), bf16[8,128,192]{1,2,0:T(8,128)(2,1)S(1)}, u32[]{:S(2)}, u32[]{:S(2)}) async-start(bf16[8,128,192]{1,2,0:T(8,128)(2,1)} %copy.24), calls=%async_computation | async-start | bytes 786432 | tf_op jit(solution)/shard_map/all_to_all | solution.py:131
  129.6 13.3 %all-to-all-start.1 = ((bf16[8,16,2560]{2,1,0:T(8,128)(2,1)}), bf16[8,16,2560]{2,1,0:T(8,128)(2,1)S(1)}, u32[]{:S(2)}, u32[]{:S(2)}) async-start(bf16[8,16,2560]{2,1,0:T(8,128)(2,1)} %bitcast.120), calls=%async_computation.1 | async-start | bytes 1310720 | tf_op jit(solution)/shard_map/all_to_all | solution.py:164
  142.9 14.1 %copy-start.2 = (bf16[8,16,2560]{2,1,0:T(8,128)(2,1)}, bf16[8,16,2560]{2,1,0:T(8,128)(2,1)S(1)}, u32[]{:S(2)}) copy-start(bf16[8,16,2560]{2,1,0:T(8,128)(2,1)S(1)} %all-to-all-done.1) | copy-start | bytes 1966084
  142.9 14.1 %all-to-all-start.3 = ((bf16[8,16,2560]{2,1,0:T(8,128)(2,1)}), bf16[8,16,2560]{2,1,0:T(8,128)(2,1)}, u32[]{:S(2)}, u32[]{:S(2)}) async-start(bf16[8,16,2560]{2,1,0:T(8,128)(2,1)} %bitcast.122), calls=%async_computation.3 | async-start | bytes 1310720 | tf_op jit(solution)/shard_map/all_to_all | solution.py:165
  147.1 412.5 %reduce-scatter.4.cloned.1.call-start = ((), (), s32[]{:S(2)}) async-start(), calls=%async_computation.11 | async-start | bytes 5570560 | tf_op jit(solution)/shard_map/reduce_scatter | solution.py:182
  183.1 4.6 copy-start.3
  183.1 4.6 copy-start.5
  191.6 439.0 %reduce-scatter.6.cloned.1.call-start = ((), (), s32[]{:S(2)}) async-start(), calls=%async_computation.12 | async-start | bytes 5570560 | tf_op jit(solution)/shard_map/reduce_scatter | solution.py:185
  196.7 504.5 %reduce-scatter.8.cloned.1.call-start = ((), (), s32[]{:S(2)}) async-start(), calls=%async_computation.13 | async-start | bytes 5570560 | tf_op jit(solution)/shard_map/reduce_scatter | solution.py:188
Sparse Core Ops, SparseCore 0:
  9.7 41.0 all-gather.4
  52.5 39.3 all-gather.6
  93.6 45.1 all-gather.8
  140.4 42.6 all-gather.10
  191.7 367.7 reduce-scatter.3
  562.4 68.1 reduce-scatter.5
  633.6 67.5 reduce-scatter.7
where the time goes:
time: 714 us; the launch traced here: 708 us
  waiting for transfers between devices  559 us (78%)
  matrix products  68.5 us (10%)
  local copies, waits for them, and re-layouts  20.3 us (3%)
  blocking collectives  18.9 us (3%)
  starting transfers between devices  14.3 us (2%)
  between operations  14.3 us (2%)
  other arithmetic  9.83 us (1%)
    reduce_scatter x1, waiting for transfers between devices, local(): lax.psum_scatter(partial_gate[None].astype(jnp.bfloat16), 'seq', scatter_...  334 us
    reduce_scatter x1, waiting for transfers between devices, local(): lax.psum_scatter(partial_up[None].astype(jnp.bfloat16), 'seq', scatter_di...  71 us
    reduce_scatter x1, waiting for transfers between devices, local(): lax.psum_scatter(partial_down[None].astype(jnp.bfloat16), 'seq', scatter_...  70.5 us
    all_gather x1, waiting for transfers between devices, attend(): shard_rows = lax.all_gather(keyvals, 'seq', axis=0, tiled=True)  37.5 us
    all_gather x1, waiting for transfers between devices, fetch_weights(): lax.all_gather(w_down, 'seq', axis=1, tiled=True)  26.1 us
    dot_general x4, matrix products, compute(): jnp.einsum('kgqn,nkd->qkgd', weights.astype(jnp.bfloat16), value_rows, pr...  20.2 us
    all_to_all x1, blocking collectives, local(): lax.all_to_all(expert_out.reshape(expert_count, capacity, model_width), '...  18.9 us
    dot_general x4, matrix products, contract_rows(): lax.dot_general(first_operand, second_operand, (((0,), (0,)), ((), ())),...  15 us
  transfers between devices with their start and end apart: 10, of which 7 were waited for; matrix products, arithmetic and copies ran while one was open for 11% of the time, Pallas kernels for 0%

commit v1 on v0

v1 whole, which is shorter than its diff:
```python
import functools
import math

import jax
import jax.numpy as jnp
from jax import lax
from jax.experimental import pallas as pl
from jax.experimental.pallas import tpu as pltpu
from jax.sharding import Mesh
from jax.sharding import PartitionSpec as P

HEAD_DIM = 64
SEQ = ("zl", "y", "c")
UNITS = ("zl", "c")
score_to_log2 = math.log2(math.e) / math.sqrt(HEAD_DIM)
very_negative = -1e30
norm_eps = 1e-05


def contract_rows(first_operand, second_operand):
    return lax.dot_general(
        first_operand, second_operand, (((0,), (0,)), ((), ())), preferred_element_type=jnp.float32
    )


def contract_cols(first_operand, second_operand):
    return lax.dot_general(
        first_operand, second_operand, (((1,), (1,)), ((), ())), preferred_element_type=jnp.float32
    )


def swiglu_forward(gate_act, up_act):
    sigmoid_gate = jax.nn.sigmoid(gate_act)
    silu_gate = gate_act * sigmoid_gate
    return (silu_gate * up_act).astype(jnp.bfloat16)


def swiglu_backward(gate_act, up_act, hidden_grad):
    sigmoid_gate = jax.nn.sigmoid(gate_act)
    silu_gate = gate_act * sigmoid_gate
    gate_grad = (
        hidden_grad * up_act * sigmoid_gate * (1.0 + gate_act * (1.0 - sigmoid_gate))
    ).astype(jnp.bfloat16)
    up_grad = (hidden_grad * silu_gate).astype(jnp.bfloat16)
    return (gate_grad, up_grad)


def attention_kernel(place, q_ref, kv_ref, out_ref, m_ref, acc_ref):
    half_rows = out_ref.shape[1]
    heads = out_ref.shape[2] // HEAD_DIM
    shard_rows = 2 * half_rows
    pieces = half_rows // 128
    ones = jnp.ones((16, half_rows), jnp.bfloat16)

    def values_of(block, part):
        turned = [
            kv_ref[block, pl.ds(half_rows + (part * pieces + j) * HEAD_DIM, HEAD_DIM), :]
            for j in range(pieces)
        ]
        return jnp.concatenate([jnp.concatenate(turned, axis=1), ones], axis=0)

    def step(half, block, parts, masked):
        keys = kv_ref[block, pl.ds(0, half_rows), :]
        scores = []
        for part in range(parts):
            s = (
                jnp.dot(keys, q_ref[half, part], preferred_element_type=jnp.float32)
                * score_to_log2
            )
            if masked and part == parts - 1:
                key_place = lax.broadcasted_iota(jnp.int32, s.shape, 0)
                query_place = lax.broadcasted_iota(jnp.int32, s.shape, 1) % half_rows
                s = jnp.where(key_place <= query_place, s, very_negative)
            scores.append(s)
        old = m_ref[...]
        new = old
        for s in scores:
            new = jnp.maximum(new, jnp.max(s, axis=0, keepdims=True))
        m_ref[...] = new
        total = acc_ref[...] * jnp.exp2(old - new)
        for part, s in enumerate(scores):
            weights = jnp.exp2(s - new).astype(jnp.bfloat16)
            total += jnp.dot(values_of(block, part), weights, preferred_element_type=jnp.float32)
        acc_ref[...] = total

    def run(half, full_blocks, last_parts):
        m_ref[...] = jnp.full_like(m_ref, very_negative)
        acc_ref[...] = jnp.zeros_like(acc_ref)

        def body(block, carry):
            step(half, block, 2, False)
            return carry

        lax.fori_loop(0, full_blocks, body, 0)
        step(half, full_blocks, last_parts, True)
        mixed = acc_ref[pl.ds(0, HEAD_DIM), :] / acc_ref[pl.ds(HEAD_DIM, 1), :]
        for head in range(heads):
            out_ref[half, :, pl.ds(head * HEAD_DIM, HEAD_DIM)] = (
                mixed[:, head * half_rows : (head + 1) * half_rows].T.astype(jnp.bfloat16)
            )

    shard = place[0]
    mirror = place[1]
    run(1, mirror, 2)
    run(0, shard, 1)


def attend(queries, keyvals):
    row_count = queries.shape[0]
    half_rows = row_count // 2
    heads = queries.shape[1] // HEAD_DIM
    shard_count = lax.axis_size(SEQ)
    shard = lax.axis_index(SEQ)
    swap = [(s, shard_count - 1 - s) for s in range(shard_count)]
    keys = keyvals[:, :HEAD_DIM]
    keys = jnp.concatenate([keys[:half_rows], keys[half_rows:]], axis=1)
    values = keyvals[:, HEAD_DIM:].reshape(row_count // 128, 128, HEAD_DIM)
    values = jnp.transpose(values, (0, 2, 1)).reshape(half_rows, 2 * HEAD_DIM)
    packed = jnp.concatenate([keys, values], axis=0)
    gathered = lax.all_gather(packed, SEQ, axis=0, tiled=False)
    odd = lax.ppermute(queries[half_rows:], SEQ, swap)

    def turn(rows):
        turned = jnp.transpose(rows.reshape(half_rows, heads, HEAD_DIM), (2, 1, 0)).reshape(
            HEAD_DIM, heads * half_rows
        )
        empty = jnp.zeros_like(turned)
        return jnp.stack(
            [jnp.concatenate([turned, empty], axis=0), jnp.concatenate([empty, turned], axis=0)]
        )

    turned_queries = jnp.stack([turn(queries[:half_rows]), turn(odd)])
    place = jnp.stack([shard, shard_count - 1 - shard]).astype(jnp.int32)
    mixed = pl.pallas_call(
        attention_kernel,
        out_shape=jax.ShapeDtypeStruct((2, half_rows, heads * HEAD_DIM), jnp.bfloat16),
        in_specs=[
            pl.BlockSpec(memory_space=pltpu.SMEM),
            pl.BlockSpec(memory_space=pltpu.VMEM),
            pl.BlockSpec(memory_space=pltpu.VMEM),
        ],
        out_specs=pl.BlockSpec(memory_space=pltpu.VMEM),
        scratch_shapes=[
            pltpu.VMEM((1, heads * half_rows), jnp.float32),
            pltpu.VMEM((HEAD_DIM + 16, heads * half_rows), jnp.float32),
        ],
        compiler_params=pltpu.CompilerParams(vmem_limit_bytes=48 * 2**20),
        cost_estimate=pl.CostEstimate(
            flops=20_000_000_000, bytes_accessed=6_000_000, transcendentals=27_000_000
        ),
        name="attention",
    )(place, turned_queries, gathered)
    back = lax.ppermute(mixed[1], SEQ, swap)
    return jnp.concatenate([mixed[0], back], axis=0)


def local(
    resid,
    queries,
    keyvals,
    out_proj,
    norm_gain,
    token_ids,
    hash_table,
    w_gate,
    w_up,
    w_down,
    cotangent,
):
    token_count = resid.shape[0]
    model_width = resid.shape[1]
    expert_count = lax.axis_size("exp")
    capacity = token_count // expert_count
    expert_of = jnp.take(hash_table, token_ids)
    onehot_slots = (
        expert_of[:, None] == jnp.arange(expert_count, dtype=jnp.int32)[None, :]
    ).astype(jnp.int32)
    earlier = jnp.cumsum(onehot_slots, axis=0) - onehot_slots
    slot_of = jnp.sum(onehot_slots * earlier, axis=1)
    target = jnp.where(slot_of < capacity, expert_of * capacity + slot_of, -1)
    dispatch_table = (
        jnp.arange(expert_count * capacity, dtype=jnp.int32)[:, None] == target[None, :]
    ).astype(jnp.bfloat16)

    def to_experts(rows):
        sent = (
            jnp.dot(dispatch_table, rows, preferred_element_type=jnp.float32)
            .astype(jnp.bfloat16)
            .reshape(expert_count, capacity, model_width)
        )
        routed = lax.all_to_all(sent, "exp", split_axis=0, concat_axis=0, tiled=True)
        return lax.all_gather(
            routed.reshape(expert_count * capacity, model_width), "y", axis=0, tiled=True
        )

    attention = attend(queries, keyvals)
    output_grads = to_experts(cotangent)
    full_gate, full_up, full_down = (
        lax.all_gather(w[0], UNITS, axis=0, tiled=True) for w in (w_gate, w_up, w_down)
    )
    token_heads = lax.all_to_all(attention, "exp", split_axis=0, concat_axis=1, tiled=True)
    projected = jnp.dot(token_heads, out_proj, preferred_element_type=jnp.float32)
    hidden_state = (resid.astype(jnp.float32) + projected).astype(jnp.bfloat16)
    widened = hidden_state.astype(jnp.float32)
    mean_square = jnp.mean(widened * widened, axis=1, keepdims=True)
    normed = (widened * lax.rsqrt(mean_square + norm_eps) * norm_gain.astype(jnp.float32)).astype(
        jnp.bfloat16
    )
    expert_rows = to_experts(normed)
    gate_act = contract_cols(expert_rows, full_gate)
    up_act = contract_cols(expert_rows, full_up)
    hidden_units = swiglu_forward(gate_act, up_act)
    expert_out = jnp.dot(hidden_units, full_down, preferred_element_type=jnp.float32).astype(
        jnp.bfloat16
    )
    summed_out = lax.psum_scatter(expert_out, "y", scatter_dimension=0, tiled=True)
    hidden_grad = contract_cols(output_grads, full_down)
    gate_grad, up_grad = swiglu_backward(gate_act, up_act, hidden_grad)

    def to_owner(partial):
        return lax.psum_scatter(
            partial.astype(jnp.bfloat16), UNITS, scatter_dimension=0, tiled=True
        )[None]

    grad_gate = to_owner(contract_rows(gate_grad, expert_rows))
    grad_up = to_owner(contract_rows(up_grad, expert_rows))
    grad_down = to_owner(contract_rows(hidden_units, output_grads))
    returned_rows = lax.all_to_all(
        summed_out.reshape(expert_count, capacity, model_width),
        "exp",
        split_axis=0,
        concat_axis=0,
        tiled=True,
    )
    combined_output = contract_rows(
        dispatch_table, returned_rows.reshape(expert_count * capacity, model_width)
    )
    layer_out = (widened + combined_output).astype(jnp.bfloat16)
    return (layer_out, grad_gate, grad_up, grad_down)


def solution(mesh):
    fine_mesh = Mesh(mesh.devices.reshape(2, 4, 2, 8), ("zl", "y", "c", "exp"))
    token_spec = P((*SEQ, "exp"), None)
    weight_spec = P("exp", SEQ, None)
    in_specs = (
        token_spec,
        P(SEQ, "exp"),
        P(SEQ, "exp"),
        P(),
        P(),
        P((*SEQ, "exp")),
        P(),
        weight_spec,
        weight_spec,
        weight_spec,
        token_spec,
    )
    out_specs = (token_spec, weight_spec, weight_spec, weight_spec)
    return jax.shard_map(
        local, mesh=fine_mesh, in_specs=in_specs, out_specs=out_specs, check_vma=False
    )
```

time: 714 us -> 382 us (0.54)
  waiting for transfers between devices: 559 us -> 225 us
  Pallas kernels: 0 us -> 39.9 us
  matrix products: 68.5 us -> 31 us
  blocking collectives: 18.9 us -> 49.2 us
  local copies, waits for them, and re-layouts: 20.3 us -> 5.05 us
  other arithmetic: 9.83 us -> 1.72 us
    reduce_scatter x3 -> x4, waiting for transfers between devices: 476 us -> 79.9 us  [the longest x3 57.6 us: to_owner(): lax.psum_scatter(partial.astype(jnp.bfloat16), UNITS, scatter_dimension=0...]
    all_gather x4 -> x6, waiting for transfers between devices: 63.7 us -> 123 us  [the longest x2 49.4 us: to_experts(): lax.all_gather(routed.reshape(expert_count * capacity, model_width), 'y',...]
    pallas_call x0 -> x1, Pallas kernels: none -> 39.9 us  [attend(): pl.pallas_call(attention_kernel, out_shape=jax.ShapeDtypeStruct((2, half_...]
    all_to_all x1 -> x3, blocking collectives: 18.9 us -> 49.2 us  [the longest x2 30.2 us: to_experts(): lax.all_to_all(sent, 'exp', split_axis=0, concat_axis=0, tiled=True)]
    dot_general x11 -> x3, matrix products: 34.7 us -> 4.4 us  [the longest x1 3.66 us: local(): jnp.dot(hidden_units, full_down, preferred_element_type=jnp.float32)]
    ppermute x0 -> x2, waiting for transfers between devices: none -> 11.5 us  [the longest x1 8.41 us: attend(): back = lax.ppermute(mixed[1], SEQ, swap)]
    cond x36 -> x0, local copies, waits for them, and re-layouts: 10.7 us -> none
    all_to_all x2 -> x0, waiting for transfers between devices: 8.58 us -> none  [the longest x1 8.58 us: local(): lax.all_to_all(send_rows, 'exp', split_axis=0, concat_axis=0, tiled=True)]
  transfers between devices with their start and end apart: 10 -> 13, of which waited for: 7 -> 12; matrix products, arithmetic and copies ran while one was open for 11% -> 9% of each run, Pallas kernels for 0% -> 10%
where the time goes in v1:
time: 382 us; the launch traced here: 381 us
  waiting for transfers between devices  225 us (59%)
  blocking collectives  49.2 us (13%)
  Pallas kernels  39.9 us (10%)
  matrix products  31 us (8%)
  starting transfers between devices  14.5 us (4%)
  between operations  14.4 us (4%)
  local copies, waits for them, and re-layouts  5.05 us (1%)
    reduce_scatter x3, waiting for transfers between devices, to_owner(): lax.psum_scatter(partial.astype(jnp.bfloat16), UNITS, scatter_dimension=0...  57.6 us
    all_gather x2, waiting for transfers between devices, to_experts(): lax.all_gather(routed.reshape(expert_count * capacity, model_width), 'y',...  49.4 us
    all_gather x3, waiting for transfers between devices, local(): lax.all_gather(w[0], UNITS, axis=0, tiled=True)  43.2 us
    pallas_call x1, Pallas kernels, attend(): pl.pallas_call(attention_kernel, out_shape=jax.ShapeDtypeStruct((2, half_...  39.9 us
    all_to_all x2, blocking collectives, to_experts(): lax.all_to_all(sent, 'exp', split_axis=0, concat_axis=0, tiled=True)  30.2 us
    all_gather x1, waiting for transfers between devices, attend(): gathered = lax.all_gather(packed, SEQ, axis=0, tiled=False)  30.2 us
    reduce_scatter x1, waiting for transfers between devices, local(): lax.psum_scatter(expert_out, 'y', scatter_dimension=0, tiled=True)  22.3 us
    all_to_all x1, blocking collectives, local(): lax.all_to_all(summed_out.reshape(expert_count, capacity, model_width), '...  19 us
  transfers between devices with their start and end apart: 13, of which 12 were waited for; matrix products, arithmetic and copies ran while one was open for 9% of the time, Pallas kernels for 10%

profile of v1, /device:TPU:1, one launch (start us, length us, event | category | flops | bytes accessed | tf_op | source)
XLA Modules:
  0.0 380.9 jit_solution(7951528584803988261)
XLA Ops:
  7.2 0.0 all-gather.15.cloned.1.call-start
  7.2 1.2 slice.28
  8.4 1.0 fusion.22
  9.4 0.1 copy.20
  9.6 0.8 pad_maximum_fusion.2
  10.4 0.0 all-gather.15.cloned.1.call-update
  10.4 0.0 all-gather.17.cloned.1.call-start
  10.5 5.6 %collective-permute-start = (bf16[512,192]{0,1:T(8,128)(2,1)S(1)}, bf16[512,192]{0,1:T(8,128)(2,1)S(1)}, u32[]{:S(2)}, u32[]{:S(2)}) collective-permute-start(bf16[512,192]{0,1:T(8,128)(2,1)S(1)} %get-tuple-element.7), channel_id=1, source_target_pairs={{0,120},{8,112},{16,104},{24,96},{32,88},{40,80},{48,72},{56,64},{... | collective-permute-start | bytes 589832 | tf_op jit(solution)/shard_map/ppermute | solution.py:121
  16.1 0.0 all-gather.17.cloned.1.call-update
  16.1 0.2 copy.18
  16.4 0.1 pad_add_fusion.place
  16.5 1.1 gather_fusion
  17.6 0.1 pad_bitcast_fusion.3
  17.7 3.1 collective-permute-done
  20.8 0.2 copy.19
  21.0 0.1 pad_bitcast_fusion.1
  21.1 0.1 maximum_bitcast_fusion
  21.2 0.1 pad_maximum_fusion.q_ref
  21.4 30.2 %all-gather.15.cloned.1.call-done = bf16[16384,128]{1,0:T(8,128)(2,1)} async-done(((bf16[1024,128]{1,0:T(8,128)(2,1)}), bf16[16384,128]{1,0:T(8,128)(2,1)}) %all-gather.15.cloned.1.call-update) | async-done | bytes 4194320 | tf_op jit(solution)/shard_map/all_gather | solution.py:120
  51.6 39.9 %attention.1 = bf16[2,512,192]{2,1,0:T(8,128)(2,1)S(1)} custom-call(s32[2]{0:T(128)S(1)} %pad_add_fusion.place, bf16[2,2,128,1536]{3,2,1,0:T(8,128)(2,1)S(1)} %pad_maximum_fusion.q_ref, bf16[16,1024,128]{2,1,0:T(8,128)(2,1)} %bitcast.85), custom_call_target="tpu_custom_call" | custom-call | flops 20000000000 | bytes 6000000 | tf_op jit(solution)/shard_map/attention/pallas_call | solution.py:134
  91.5 2.0 collective-permute-start.1
  93.5 8.4 %collective-permute-done.1 = bf16[512,192]{1,0:T(8,128)(2,1)S(1)} collective-permute-done((bf16[512,192]{1,0:T(8,128)(2,1)S(1)}, bf16[512,192]{1,0:T(8,128)(2,1)S(1)}, u32[]{:S(2)}, u32[]{:S(2)}) %collective-permute-start.1) | collective-permute-done | bytes 196640 | tf_op jit(solution)/shard_map/ppermute | solution.py:153
  101.9 0.1 pad_maximum_fusion.1
  102.0 1.0 copy.21
  102.9 6.4 %all-to-all-start = ((bf16[8,128,192]{1,2,0:T(8,128)(2,1)}), bf16[8,128,192]{1,2,0:T(8,128)(2,1)S(1)}, u32[]{:S(2)}, u32[]{:S(2)}) async-start(bf16[8,128,192]{1,2,0:T(8,128)(2,1)} %copy.21), calls=%async_computation | async-start | bytes 786432 | tf_op jit(solution)/shard_map/all_to_all | solution.py:201
  109.3 0.2 all-gather.11.cloned.1.call-start
  109.5 0.1 fusion.15
  109.6 0.2 reduce_window_sum.11
  109.8 0.2 select_reduce_fusion
  110.0 9.6 %all-to-all-done = bf16[8,128,192]{1,2,0:T(8,128)(2,1)S(1)} async-done(((bf16[8,128,192]{1,2,0:T(8,128)(2,1)}), bf16[8,128,192]{1,2,0:T(8,128)(2,1)S(1)}, u32[]{:S(2)}, u32[]{:S(2)}) %all-to-all-start) | async-done | bytes 393248 | tf_op jit(solution)/shard_map/all_to_all | solution.py:201
  119.6 4.5 %multiply_reduce_fusion = (f32[128]{0:T(128)S(1)}, f32[128,2560]{1,0:T(8,128)S(1)}) fusion(bf16[128,1536]{0,1:T(8,128)(2,1)S(1)} %bitcast.74, bf16[1536,2560]{1,0:T(8,128)(2,1)} %param.14, bf16[128,2560]{1,0:T(8,128)(2,1)S(1)} %copy-done.2), kind=kOutput, calls=%fused_computation.21 | convolution fusion | flops 1008598912 | bytes 10224128 | tf_op jit(solution)/shard_map/dot_general | solution.py:202
  124.2 0.4 convolution_convert_fusion.5
  124.6 15.7 %all_to_all.34 = bf16[8,16,2560]{2,1,0:T(8,128)(2,1)} all-to-all(bf16[8,16,2560]{2,1,0:T(8,128)(2,1)S(1)} %bitcast.69), channel_id=1, replica_groups=mesh['zl'=2,'y'=4,'c'=2,'exp'=8] {'exp'}, dimensions={0} | all-to-all | bytes 1310720 | tf_op jit(solution)/shard_map/all_to_all | solution.py:191
  140.3 0.0 all-gather.11.cloned.1.call-update
  140.3 0.0 all-gather.19.cloned.1.call-start
  140.4 0.5 all-gather.19.cloned.1.call-update
  140.9 0.0 all-gather.21.cloned.1.call-start
  141.0 0.5 all-gather.21.cloned.1.call-update
  141.5 0.0 all-gather.13.cloned.1.call-start
  141.5 0.3 convolution_convert_fusion.4
  141.9 14.5 %all_to_all.35 = bf16[8,16,2560]{2,1,0:T(8,128)(2,1)} all-to-all(bf16[8,16,2560]{2,1,0:T(8,128)(2,1)S(1)} %bitcast.72), channel_id=1, replica_groups=mesh['zl'=2,'y'=4,'c'=2,'exp'=8] {'exp'}, dimensions={0} | all-to-all | bytes 1310720 | tf_op jit(solution)/shard_map/all_to_all | solution.py:191
  156.4 0.0 all-gather.13.cloned.1.call-update
  156.4 0.0 reduce-scatter.5.cloned.1.call-start
  156.5 0.0 all-gather.17.cloned.1.call-done
  156.5 15.9 %all-gather.11.cloned.1.call-done = bf16[512,2560]{1,0:T(8,128)(2,1)} async-done(((bf16[128,2560]{1,0:T(8,128)(2,1)}), bf16[512,2560]{1,0:T(8,128)(2,1)}) %all-gather.11.cloned.1.call-update) | async-done | bytes 2621456 | tf_op jit(solution)/shard_map/all_gather | solution.py:192
  172.4 3.0 fusion.8
  175.4 21.8 %all-gather.19.cloned.1.call-done = bf16[1,256,2560]{2,1,0:T(8,128)(2,1)} async-done(((bf16[1,64,2560]{2,1,0:T(8,128)(2,1)}), bf16[1,256,2560]{2,1,0:T(8,128)(2,1)}) %all-gather.19.cloned.1.call-update) | async-done | bytes 1310736 | tf_op jit(solution)/shard_map/all_gather | solution.py:199
  197.1 3.8 multiply_convert_fusion.4
  200.9 21.4 %all-gather.21.cloned.1.call-done = bf16[1,256,2560]{2,1,0:T(8,128)(2,1)} async-done(((bf16[1,64,2560]{2,1,0:T(8,128)(2,1)}), bf16[1,256,2560]{2,1,0:T(8,128)(2,1)}) %all-gather.21.cloned.1.call-update) | async-done | bytes 1310736 | tf_op jit(solution)/shard_map/all_gather | solution.py:199
  222.3 3.7 convolution_convert_fusion
  226.0 0.0 reduce-scatter.7.cloned.1.call-start
  226.1 33.6 %all-gather.13.cloned.1.call-done = bf16[512,2560]{1,0:T(8,128)(2,1)} async-done(((bf16[128,2560]{1,0:T(8,128)(2,1)}), bf16[512,2560]{1,0:T(8,128)(2,1)}) %all-gather.13.cloned.1.call-update) | async-done | bytes 2621456 | tf_op jit(solution)/shard_map/all_gather | solution.py:192
  259.6 3.1 fusion.3
  262.8 3.2 convolution_convert_fusion.3
  266.0 0.0 reduce-scatter.9.cloned.1.call-start
  266.0 3.7 convolution_convert_fusion.2
  269.8 0.0 reduce-scatter.11.cloned.1.call-start
  269.8 4.1 %convolution_convert_fusion.1 = bf16[256,2560]{1,0:T(8,128)(2,1)} fusion(bf16[512,256]{1,0:T(8,128)(2,1)S(1)} %get-tuple-element.16, bf16[512,2560]{1,0:T(8,128)(2,1)} %all-gather.13.cloned.1.call-done), kind=kOutput, calls=%fused_computation.2 | convolution fusion | flops 671744000 | bytes 4194304 | tf_op jit(solution)/shard_map/dot_general | solution.py:21
  273.9 22.3 %reduce-scatter.5.cloned.1.call-done = bf16[128,2560]{1,0:T(8,128)(2,1)} async-done(((bf16[512,2560]{1,0:T(8,128)(2,1)}), bf16[128,2560]{1,0:T(8,128)(2,1)}) %reduce-scatter.5.cloned.1.call-update) | async-done | bytes 655376 | tf_op jit(solution)/shard_map/reduce_scatter | solution.py:216
  296.2 19.0 %all_to_all.36 = bf16[8,16,2560]{2,1,0:T(8,128)(2,1)S(1)} all-to-all(bf16[8,16,2560]{2,1,0:T(8,128)(2,1)} %bitcast.82), channel_id=1, replica_groups=mesh['zl'=2,'y'=4,'c'=2,'exp'=8] {'exp'}, dimensions={0} | all-to-all | bytes 1310720 | tf_op jit(solution)/shard_map/all_to_all | solution.py:228
  315.2 1.2 fusion.2
  316.4 7.9 %reduce-scatter.7.cloned.1.call-done = bf16[64,2560]{1,0:T(8,128)(2,1)} async-done(((bf16[256,2560]{1,0:T(8,128)(2,1)}), bf16[64,2560]{1,0:T(8,128)(2,1)}) %reduce-scatter.7.cloned.1.call-update) | async-done | bytes 327696 | tf_op jit(solution)/shard_map/reduce_scatter | solution.py:221
  324.4 24.0 %reduce-scatter.9.cloned.1.call-done = bf16[64,2560]{1,0:T(8,128)(2,1)} async-done(((bf16[256,2560]{1,0:T(8,128)(2,1)}), bf16[64,2560]{1,0:T(8,128)(2,1)}) %reduce-scatter.9.cloned.1.call-update) | async-done | bytes 327696 | tf_op jit(solution)/shard_map/reduce_scatter | solution.py:221
  348.4 25.7 %reduce-scatter.11.cloned.1.call-done = bf16[64,2560]{1,0:T(8,128)(2,1)} async-done(((bf16[256,2560]{1,0:T(8,128)(2,1)}), bf16[64,2560]{1,0:T(8,128)(2,1)}) %reduce-scatter.11.cloned.1.call-update) | async-done | bytes 327696 | tf_op jit(solution)/shard_map/reduce_scatter | solution.py:221
  (28 shorter events, 0.3 us)
Async XLA Ops:
  7.2 134.4 %copy-start = (bf16[128,2560]{1,0:T(8,128)(2,1)S(1)}, bf16[128,2560]{1,0:T(8,128)(2,1)}, u32[]{:S(2)}) copy-start(bf16[128,2560]{1,0:T(8,128)(2,1)} %param.21) | copy-start | bytes 1966084
  7.2 3.3 copy-start.4
  7.2 44.4 %all-gather.15.cloned.1.call-start = ((), (), s32[]{:S(2)}) async-start(), calls=%async_computation.14 | async-start | bytes 4456448 | tf_op jit(solution)/shard_map/all_gather | solution.py:120
  10.4 5.9 %copy-start.6 = (s32[128]{0:T(128)S(1)}, s32[128]{0:T(128)}, u32[]{:S(2)}) copy-start(s32[128]{0:T(128)} %param.16) | copy-start | bytes 1540
  10.4 6.1 %copy-start.3 = (s32[128256]{0:T(1024)S(1)}, s32[128256]{0:T(1024)}, u32[]{:S(2)}) copy-start(s32[128256]{0:T(1024)} %param.17) | copy-start | bytes 1539076
  10.4 146.1 %all-gather.17.cloned.1.call-start = ((), (), s32[]{:S(2)}) async-start(), calls=%async_computation.15 | async-start | bytes 1638400 | tf_op jit(solution)/shard_map/all_gather | solution.py:199
  10.5 10.3 %collective-permute-start = (bf16[512,192]{0,1:T(8,128)(2,1)S(1)}, bf16[512,192]{0,1:T(8,128)(2,1)S(1)}, u32[]{:S(2)}, u32[]{:S(2)}) collective-permute-start(bf16[512,192]{0,1:T(8,128)(2,1)S(1)} %get-tuple-element.7), channel_id=1, source_target_pairs={{0,120},{8,112},{16,104},{24,96},{32,88},{40,80},{48,72},{56,64},{... | collective-permute-start | bytes 589832 | tf_op jit(solution)/shard_map/ppermute | solution.py:121
  91.5 10.4 %collective-permute-start.1 = (bf16[512,192]{1,0:T(8,128)(2,1)S(1)}, bf16[512,192]{1,0:T(8,128)(2,1)S(1)}, u32[]{:S(2)}, u32[]{:S(2)}) collective-permute-start(bf16[512,192]{1,0:T(8,128)(2,1)S(1)} %get-tuple-element.5), channel_id=1, source_target_pairs={{0,120},{8,112},{16,104},{24,96},{32,88},{40,80},{48,72},{56,64},{... | collective-permute-start | bytes 589832 | tf_op jit(solution)/shard_map/ppermute | solution.py:153
  101.9 7.7 %copy-start.5 = (bf16[2560]{0:T(1024)(128)(2,1)S(1)}, bf16[2560]{0:T(1024)(128)(2,1)}, u32[]{:S(2)}) copy-start(bf16[2560]{0:T(1024)(128)(2,1)} %param.15) | copy-start | bytes 15364
  101.9 17.7 %copy-start.2 = (bf16[128,2560]{1,0:T(8,128)(2,1)S(1)}, bf16[128,2560]{1,0:T(8,128)(2,1)}, u32[]{:S(2)}) copy-start(bf16[128,2560]{1,0:T(8,128)(2,1)} %param.11) | copy-start | bytes 1966084
  102.9 16.7 %all-to-all-start = ((bf16[8,128,192]{1,2,0:T(8,128)(2,1)}), bf16[8,128,192]{1,2,0:T(8,128)(2,1)S(1)}, u32[]{:S(2)}, u32[]{:S(2)}) async-start(bf16[8,128,192]{1,2,0:T(8,128)(2,1)} %copy.21), calls=%async_computation | async-start | bytes 786432 | tf_op jit(solution)/shard_map/all_to_all | solution.py:201
  109.3 63.1 %all-gather.11.cloned.1.call-start = ((), (), s32[]{:S(2)}) async-start(), calls=%async_computation.8 | async-start | bytes 3276800 | tf_op jit(solution)/shard_map/all_gather | solution.py:192
  140.3 56.8 %all-gather.19.cloned.1.call-start = ((), (), s32[]{:S(2)}) async-start(), calls=%async_computation.16 | async-start | bytes 1638400 | tf_op jit(solution)/shard_map/all_gather | solution.py:199
  140.9 81.4 %all-gather.21.cloned.1.call-start = ((), (), s32[]{:S(2)}) async-start(), calls=%async_computation.17 | async-start | bytes 1638400 | tf_op jit(solution)/shard_map/all_gather | solution.py:199
  141.5 118.1 %all-gather.13.cloned.1.call-start = ((), (), s32[]{:S(2)}) async-start(), calls=%async_computation.10 | async-start | bytes 3276800 | tf_op jit(solution)/shard_map/all_gather | solution.py:192
  156.4 139.8 %reduce-scatter.5.cloned.1.call-start = ((), (), s32[]{:S(2)}) async-start(), calls=%async_computation.9 | async-start | bytes 3276800 | tf_op jit(solution)/shard_map/reduce_scatter | solution.py:216
  226.0 98.3 %reduce-scatter.7.cloned.1.call-start = ((), (), s32[]{:S(2)}) async-start(), calls=%async_computation.11 | async-start | bytes 1638400 | tf_op jit(solution)/shard_map/reduce_scatter | solution.py:221
  259.6 3.1 copy-start.1
  266.0 82.4 %reduce-scatter.9.cloned.1.call-start = ((), (), s32[]{:S(2)}) async-start(), calls=%async_computation.12 | async-start | bytes 1638400 | tf_op jit(solution)/shard_map/reduce_scatter | solution.py:221
  269.8 104.3 %reduce-scatter.11.cloned.1.call-start = ((), (), s32[]{:S(2)}) async-start(), calls=%async_computation.13 | async-start | bytes 1638400 | tf_op jit(solution)/shard_map/reduce_scatter | solution.py:221
Sparse Core Ops, SparseCore 0:
  10.5 41.0 all-gather.14
  53.2 22.7 all-gather.16
  140.4 31.8 all-gather.10
  173.9 23.2 all-gather.18
  198.6 23.6 all-gather.20
  223.8 35.7 all-gather.12
  262.0 34.1 reduce-scatter.4
  299.2 25.1 reduce-scatter.6
  327.3 20.9 reduce-scatter.8
  351.2 22.8 reduce-scatter.10

commit v2 on v1

--- a/solution.py
+++ b/solution.py
@@ -11,7 +11,8 @@
 
 HEAD_DIM = 64
 SEQ = ("zl", "y", "c")
-UNITS = ("zl", "c")
+UNITS = ("c", "y")
+MESH = pl.DeviceIdType.MESH
 score_to_log2 = math.log2(math.e) / math.sqrt(HEAD_DIM)
 very_negative = -1e30
 norm_eps = 1e-05
@@ -152,6 +153,267 @@
     )(place, turned_queries, gathered)
     back = lax.ppermute(mixed[1], SEQ, swap)
     return jnp.concatenate([mixed[0], back], axis=0)
+
+
+def neighbour(**place):
+    return {axis: place.get(axis, lax.axis_index(axis)) for axis in (*SEQ, "exp")}
+
+
+def expert_kernel(
+    rows_ref,
+    cot_ref,
+    gate_ref,
+    up_ref,
+    down_ref,
+    hidden_ref,
+    combine_ref,
+    layer_ref,
+    grad_gate_ref,
+    grad_up_ref,
+    grad_down_ref,
+    rows_in,
+    cot_in,
+    out_buf,
+    out_in,
+    parts,
+    core_in,
+    sums,
+    half_up_in,
+    half_down_in,
+    full_up_in,
+    full_down_in,
+    push_send,
+    push_recv,
+    ring_send,
+    ring_recv,
+    local_sem,
+):
+    zl, y, c, ex = (lax.axis_index(a) for a in (*SEQ, "exp"))
+    experts = rows_ref.shape[0]
+    capacity, width = rows_ref.shape[1:]
+    tokens = 2 * experts * capacity
+    core_peer = neighbour(c=1 - c)
+    y_up = neighbour(y=lax.rem(y + 1, 4))
+    y_down = neighbour(y=lax.rem(y + 3, 4))
+    offsets = [(dz, de) for dz in range(2) for de in range(experts)]
+
+    def peer(dz, de):
+        return lax.rem(zl + dz, 2), lax.rem(ex + de, experts)
+
+    def source(dz, de):
+        return lax.rem(zl + 2 - dz, 2), lax.rem(ex + experts - de, experts)
+
+    barrier = pltpu.get_barrier_semaphore()
+    for dz, de in offsets[1:]:
+        tz, te = peer(dz, de)
+        pl.semaphore_signal(
+            barrier, inc=1, device_id=neighbour(zl=tz, exp=te), device_id_type=MESH
+        )
+    for other in (core_peer, y_up, y_down):
+        pl.semaphore_signal(barrier, inc=1, device_id=other, device_id_type=MESH)
+    pl.semaphore_wait(barrier, len(offsets) + 2)
+
+    def push(kind, index, src, dst, to):
+        return pltpu.make_async_remote_copy(
+            src_ref=src,
+            dst_ref=dst,
+            send_sem=push_send.at[kind, index],
+            recv_sem=push_recv.at[kind, index],
+            device_id=to,
+            device_id_type=MESH,
+        )
+
+    def spread(kind, src_ref, dst_ref):
+        own = pltpu.make_async_copy(src_ref.at[ex], dst_ref.at[zl, ex], local_sem.at[kind])
+        own.start()
+        sent = []
+        for index, (dz, de) in enumerate(offsets):
+            if index:
+                tz, te = peer(dz, de)
+                copy = push(
+                    kind, index, src_ref.at[te], dst_ref.at[zl, ex], neighbour(zl=tz, exp=te)
+                )
+                copy.start()
+                sent.append(copy)
+        return own, sent
+
+    def arrive(spread_copies):
+        own, sent = spread_copies
+        own.wait()
+        for copy in sent:
+            copy.wait_recv()
+
+    cot_copies = spread(0, cot_ref, cot_in)
+    rows_copies = spread(1, rows_ref, rows_in)
+
+    def flat(ref):
+        return ref[...].reshape(tokens, width)
+
+    def ring(mat, stage, src, dst, to):
+        return pltpu.make_async_remote_copy(
+            src_ref=src,
+            dst_ref=dst,
+            send_sem=ring_send.at[mat, stage],
+            recv_sem=ring_recv.at[mat, stage],
+            device_id=to,
+            device_id_type=MESH,
+        )
+
+    chunk = 512
+
+    def partial(mat, first, second):
+        turned = first.T
+        for start in range(0, width, chunk):
+            part = jnp.dot(
+                turned, second[:, start : start + chunk], preferred_element_type=jnp.float32
+            ).astype(jnp.bfloat16)
+            parts[mat, :, :, :, pl.ds(start, chunk)] = part.reshape(2, 4, -1, chunk)
+
+    started = []
+
+    def go(copy):
+        copy.start()
+        started.append(copy)
+        return copy
+
+    def core_stage(mat):
+        return go(ring(mat, 0, parts.at[mat, 1 - c], core_in.at[mat], core_peer))
+
+    def wide(value):
+        return value.astype(jnp.float32)
+
+    half = parts.shape[3] // 2
+
+    def half_stage(mat, core_copy):
+        core_copy.wait_recv()
+        sums[mat] = (wide(parts[mat, c]) + wide(core_in[mat])).astype(jnp.bfloat16)
+        far = lax.rem(y + 2, 4)
+        return (
+            go(ring(mat, 1, sums.at[mat, far, pl.ds(0, half)], half_up_in.at[mat], y_up)),
+            go(ring(mat, 2, sums.at[mat, far, pl.ds(half, half)], half_down_in.at[mat], y_down)),
+        )
+
+    def full_stage(mat, copies):
+        above = lax.rem(y + 1, 4)
+        below = lax.rem(y + 3, 4)
+        copies[0].wait_recv()
+        low = pl.ds(0, half)
+        sums[mat, above, low] = (wide(sums[mat, above, low]) + wide(half_up_in[mat])).astype(
+            jnp.bfloat16
+        )
+        first = go(ring(mat, 3, sums.at[mat, above], full_up_in.at[mat], y_up))
+        copies[1].wait_recv()
+        high = pl.ds(half, half)
+        sums[mat, below, high] = (wide(sums[mat, below, high]) + wide(half_down_in[mat])).astype(
+            jnp.bfloat16
+        )
+        return (first, go(ring(mat, 4, sums.at[mat, below], full_down_in.at[mat], y_down)))
+
+    def finish(mat, copies, out_ref):
+        for copy in copies:
+            copy.wait_recv()
+        out_ref[0] = (wide(sums[mat, y]) + wide(full_up_in[mat]) + wide(full_down_in[mat])).astype(
+            jnp.bfloat16
+        )
+
+    arrive(cot_copies)
+    output_grads = flat(cot_in)
+    hidden_grad = contract_cols(output_grads, down_ref[...])
+    arrive(rows_copies)
+    expert_rows = flat(rows_in)
+    gate_act = contract_cols(expert_rows, gate_ref[...])
+    up_act = contract_cols(expert_rows, up_ref[...])
+    hidden_units = swiglu_forward(gate_act, up_act)
+    partial(0, hidden_units, output_grads)
+    core_down = core_stage(0)
+    gate_grad, up_grad = swiglu_backward(gate_act, up_act, hidden_grad)
+    partial(1, gate_grad, expert_rows)
+    core_gate = core_stage(1)
+    half_down = half_stage(0, core_down)
+    partial(2, up_grad, expert_rows)
+    core_up = core_stage(2)
+    half_gate = half_stage(1, core_gate)
+    for start in range(0, width, chunk):
+        out_buf[:, :, :, pl.ds(start, chunk)] = (
+            jnp.dot(
+                hidden_units,
+                down_ref[:, pl.ds(start, chunk)],
+                preferred_element_type=jnp.float32,
+            )
+            .astype(jnp.bfloat16)
+            .reshape(2, experts, capacity, chunk)
+        )
+    own_out = pltpu.make_async_copy(out_buf.at[zl, ex], out_in.at[zl, ex], local_sem.at[2])
+    own_out.start()
+    back = []
+    for index, (dz, de) in enumerate(offsets):
+        if index:
+            tz, te = peer(dz, de)
+            copy = push(
+                2, index, out_buf.at[tz, te], out_in.at[zl, ex], neighbour(zl=tz, exp=te)
+            )
+            copy.start()
+            back.append(copy)
+    full_down = full_stage(0, half_down)
+    half_up = half_stage(2, core_up)
+    full_gate = full_stage(1, half_gate)
+    full_up = full_stage(2, half_up)
+    finish(0, full_down, grad_down_ref)
+    arrive((own_out, back))
+    for start in range(0, width, chunk):
+        cols = pl.ds(start, chunk)
+        returned = out_in[:, :, :, cols].reshape(tokens, chunk)
+        layer_ref[:, cols] = (
+            wide(hidden_ref[:, cols])
+            + jnp.dot(combine_ref[...], returned, preferred_element_type=jnp.float32)
+        ).astype(jnp.bfloat16)
+    finish(1, full_gate, grad_gate_ref)
+    finish(2, full_up, grad_up_ref)
+    for copy in (*cot_copies[1], *rows_copies[1], *back, *started):
+        copy.wait_send()
+
+
+def expert_layer(send_rows, send_grads, weights, hidden_state, dispatch_table):
+    experts, capacity, width = send_rows.shape
+    units = weights[0].shape[0]
+    owned = units // 8
+    token_count = hidden_state.shape[0]
+    combine = jnp.concatenate([dispatch_table, dispatch_table], axis=0).T
+    vmem = pl.BlockSpec(memory_space=pltpu.VMEM)
+    bf16 = jnp.bfloat16
+    landing = pltpu.VMEM((2, experts, capacity, width), bf16)
+    grad_shape = jax.ShapeDtypeStruct((1, owned, width), bf16)
+    return pl.pallas_call(
+        expert_kernel,
+        out_shape=(jax.ShapeDtypeStruct((token_count, width), bf16),) + (grad_shape,) * 3,
+        in_specs=[vmem] * 7,
+        out_specs=(vmem,) * 4,
+        scratch_shapes=[
+            landing,
+            landing,
+            landing,
+            landing,
+            pltpu.VMEM((3, 2, 4, owned, width), bf16),
+            pltpu.VMEM((3, 4, owned, width), bf16),
+            pltpu.VMEM((3, 4, owned, width), bf16),
+            pltpu.VMEM((3, owned // 2, width), bf16),
+            pltpu.VMEM((3, owned // 2, width), bf16),
+            pltpu.VMEM((3, owned, width), bf16),
+            pltpu.VMEM((3, owned, width), bf16),
+            pltpu.SemaphoreType.DMA((3, 2 * experts)),
+            pltpu.SemaphoreType.DMA((3, 2 * experts)),
+            pltpu.SemaphoreType.DMA((3, 5)),
+            pltpu.SemaphoreType.DMA((3, 5)),
+            pltpu.SemaphoreType.DMA((3,)),
+        ],
+        compiler_params=pltpu.CompilerParams(
+            collective_id=1, has_side_effects=True, vmem_limit_bytes=56 * 2**20
+        ),
+        cost_estimate=pl.CostEstimate(
+            flops=5_000_000_000, bytes_accessed=20_000_000, transcendentals=200_000
+        ),
+        name="experts",
+    )(send_rows, send_grads, *weights, hidden_state, combine)
 
 
 def local(
@@ -182,22 +444,15 @@
         jnp.arange(expert_count * capacity, dtype=jnp.int32)[:, None] == target[None, :]
     ).astype(jnp.bfloat16)
 
-    def to_experts(rows):
-        sent = (
+    def placed(rows):
+        return (
             jnp.dot(dispatch_table, rows, preferred_element_type=jnp.float32)
             .astype(jnp.bfloat16)
             .reshape(expert_count, capacity, model_width)
         )
-        routed = lax.all_to_all(sent, "exp", split_axis=0, concat_axis=0, tiled=True)
-        return lax.all_gather(
-            routed.reshape(expert_count * capacity, model_width), "y", axis=0, tiled=True
-        )
 
     attention = attend(queries, keyvals)
-    output_grads = to_experts(cotangent)
-    full_gate, full_up, full_down = (
-        lax.all_gather(w[0], UNITS, axis=0, tiled=True) for w in (w_gate, w_up, w_down)
-    )
+    weights = [lax.all_gather(w[0], UNITS, axis=0, tiled=True) for w in (w_gate, w_up, w_down)]
     token_heads = lax.all_to_all(attention, "exp", split_axis=0, concat_axis=1, tiled=True)
     projected = jnp.dot(token_heads, out_proj, preferred_element_type=jnp.float32)
     hidden_state = (resid.astype(jnp.float32) + projected).astype(jnp.bfloat16)
@@ -206,37 +461,7 @@
     normed = (widened * lax.rsqrt(mean_square + norm_eps) * norm_gain.astype(jnp.float32)).astype(
         jnp.bfloat16
     )
-    expert_rows = to_experts(normed)
-    gate_act = contract_cols(expert_rows, full_gate)
-    up_act = contract_cols(expert_rows, full_up)
-    hidden_units = swiglu_forward(gate_act, up_act)
-    expert_out = jnp.dot(hidden_units, full_down, preferred_element_type=jnp.float32).astype(
-        jnp.bfloat16
-    )
-    summed_out = lax.psum_scatter(expert_out, "y", scatter_dimension=0, tiled=True)
-    hidden_grad = contract_cols(output_grads, full_down)
-    gate_grad, up_grad = swiglu_backward(gate_act, up_act, hidden_grad)
-
-    def to_owner(partial):
-        return lax.psum_scatter(
-            partial.astype(jnp.bfloat16), UNITS, scatter_dimension=0, tiled=True
-        )[None]
-
-    grad_gate = to_owner(contract_rows(gate_grad, expert_rows))
-    grad_up = to_owner(contract_rows(up_grad, expert_rows))
-    grad_down = to_owner(contract_rows(hidden_units, output_grads))
-    returned_rows = lax.all_to_all(
-        summed_out.reshape(expert_count, capacity, model_width),
-        "exp",
-        split_axis=0,
-        concat_axis=0,
-        tiled=True,
-    )
-    combined_output = contract_rows(
-        dispatch_table, returned_rows.reshape(expert_count * capacity, model_width)
-    )
-    layer_out = (widened + combined_output).astype(jnp.bfloat16)
-    return (layer_out, grad_gate, grad_up, grad_down)
+    return expert_layer(placed(normed), placed(cotangent), weights, hidden_state, dispatch_table)
 
 
 def solution(mesh):

time: 382 us -> 238 us (0.62)
  waiting for transfers between devices: 225 us -> 65.2 us
  Pallas kernels: 39.9 us -> 125 us
  blocking collectives: 49.2 us -> 0 us
  matrix products: 31 us -> 7.16 us
  local copies, waits for them, and re-layouts: 5.05 us -> 10.3 us
    pallas_call x0 -> x1, Pallas kernels: none -> 84.6 us  [expert_layer(): pl.pallas_call(expert_kernel, out_shape=(jax.ShapeDtypeStruct((token_coun...]
    reduce_scatter x4 -> x0, waiting for transfers between devices: 79.9 us -> none  [the longest x3 57.6 us: to_owner(): lax.psum_scatter(partial.astype(jnp.bfloat16), UNITS, scatter_dimension=0...]
    all_gather x2 -> x0, waiting for transfers between devices: 49.4 us -> none  [to_experts(): lax.all_gather(routed.reshape(expert_count * capacity, model_width), 'y',...]
    all_to_all x3 -> x0, blocking collectives: 49.2 us -> none  [the longest x2 30.2 us: to_experts(): lax.all_to_all(sent, 'exp', split_axis=0, concat_axis=0, tiled=True)]
    all_gather x3, waiting for transfers between devices: 43.2 us -> 10.2 us  [local(): lax.all_gather(w[0], UNITS, axis=0, tiled=True)]
    dot_general x10 -> x2, matrix products: 26.5 us -> 2.6 us  [placed(): jnp.dot(dispatch_table, rows, preferred_element_type=jnp.float32)]
    ppermute x1, waiting for transfers between devices: 8.41 us -> 13.9 us  [attend(): back = lax.ppermute(mixed[1], SEQ, swap)]
    unnamed x16 -> x24, local copies, waits for them, and re-layouts: 0.13 us -> 5.34 us
  transfers between devices with their start and end apart: 13 -> 7, of which waited for: 12 -> 5; matrix products, arithmetic and copies ran while one was open for 9% -> 5% of each run, Pallas kernels for 10% -> 17%
where the time goes in v2:
time: 238 us
  Pallas kernels  125 us (53%)
  waiting for transfers between devices  65.2 us (27%)
  between operations  14.1 us (6%)
  starting transfers between devices  13.9 us (6%)
  local copies, waits for them, and re-layouts  10.3 us (4%)
  matrix products  7.16 us (3%)
  other arithmetic  2.44 us (1%)
    pallas_call x1, Pallas kernels, expert_layer(): pl.pallas_call(expert_kernel, out_shape=(jax.ShapeDtypeStruct((token_coun...  84.6 us
    pallas_call x1, Pallas kernels, attend(): pl.pallas_call(attention_kernel, out_shape=jax.ShapeDtypeStruct((2, half_...  39.9 us
    all_gather x1, waiting for transfers between devices, attend(): gathered = lax.all_gather(packed, SEQ, axis=0, tiled=False)  28.7 us
    ppermute x1, waiting for transfers between devices, attend(): back = lax.ppermute(mixed[1], SEQ, swap)  13.9 us
    all_gather x3, waiting for transfers between devices, local(): lax.all_gather(w[0], UNITS, axis=0, tiled=True)  10.2 us
    all_to_all x1, waiting for transfers between devices, local(): lax.all_to_all(attention, 'exp', split_axis=0, concat_axis=1, tiled=True)  8.38 us
    all_to_all x1, starting transfers between devices, local(): lax.all_to_all(attention, 'exp', split_axis=0, concat_axis=1, tiled=True)  6.27 us
    ppermute x1, starting transfers between devices, attend(): odd = lax.ppermute(queries[half_rows:], SEQ, swap)  5.56 us
  transfers between devices with their start and end apart: 7, of which 5 were waited for; matrix products, arithmetic and copies ran while one was open for 5% of the time, Pallas kernels for 17%

profile of v2, /device:TPU:1, one launch (start us, length us, event | category | flops | bytes accessed | tf_op | source)
XLA Modules:
  0.0 237.6 jit_solution(6387933141312438549)
XLA Ops:
  7.2 0.0 copy-start
  7.2 0.0 copy-start.4
  7.2 0.0 all-gather.9.cloned.1.call-start
  7.2 1.1 fusion.12
  8.3 1.1 slice.28
  9.4 0.1 copy.20
  9.6 0.8 pad_maximum_fusion.2
  10.4 0.0 all-gather.9.cloned.1.call-update
  10.4 0.0 all-gather.11.cloned.1.call-start
  10.5 0.7 all-gather.11.cloned.1.call-update
  11.2 0.0 all-gather.13.cloned.1.call-start
  11.2 0.7 all-gather.13.cloned.1.call-update
  11.9 0.0 copy-start.8
  11.9 0.0 copy-start.3
  11.9 0.0 all-gather.15.cloned.1.call-start
  12.0 0.0 copy-done.4
  12.0 0.0 copy-start.7
  12.0 5.6 %collective-permute-start = (bf16[512,192]{0,1:T(8,128)(2,1)S(1)}, bf16[512,192]{0,1:T(8,128)(2,1)S(1)}, u32[]{:S(2)}, u32[]{:S(2)}) collective-permute-start(bf16[512,192]{0,1:T(8,128)(2,1)S(1)} %get-tuple-element.7), channel_id=1, source_target_pairs={{0,120},{8,112},{16,104},{24,96},{32,88},{40,80},{48,72},{56,64},{... | collective-permute-start | bytes 589832 | tf_op jit(solution)/shard_map/ppermute | solution.py:122
  17.6 0.0 all-gather.15.cloned.1.call-update
  17.6 0.2 copy.18
  17.8 0.1 pad_bitcast_fusion.3
  17.9 0.0 copy-done.8
  17.9 0.0 copy-done.3
  18.0 1.1 gather_fusion
  19.1 0.1 fusion.8
  19.2 0.2 reduce_window_sum.11
  19.4 0.2 select_reduce_fusion
  19.6 0.0 copy-done.7
  19.6 0.1 pad_add_fusion.place
  19.7 2.6 %collective-permute-done = bf16[512,192]{0,1:T(8,128)(2,1)S(1)} collective-permute-done((bf16[512,192]{0,1:T(8,128)(2,1)S(1)}, bf16[512,192]{0,1:T(8,128)(2,1)S(1)}, u32[]{:S(2)}, u32[]{:S(2)}) %collective-permute-start) | collective-permute-done | bytes 196640 | tf_op jit(solution)/shard_map/ppermute | solution.py:122
  22.3 0.2 copy.19
  22.5 0.1 pad_bitcast_fusion.1
  22.6 0.1 maximum_bitcast_fusion
  22.7 0.1 pad_maximum_fusion.q_ref
  22.9 28.7 %all-gather.9.cloned.1.call-done = bf16[16384,128]{1,0:T(8,128)(2,1)} async-done(((bf16[1024,128]{1,0:T(8,128)(2,1)}), bf16[16384,128]{1,0:T(8,128)(2,1)}) %all-gather.9.cloned.1.call-update) | async-done | bytes 4194320 | tf_op jit(solution)/shard_map/all_gather | solution.py:121
  51.6 39.9 %attention.1 = bf16[2,512,192]{2,1,0:T(8,128)(2,1)S(1)} custom-call(s32[2]{0:T(128)S(1)} %pad_add_fusion.place, bf16[2,2,128,1536]{3,2,1,0:T(8,128)(2,1)S(1)} %pad_maximum_fusion.q_ref, bf16[16,1024,128]{2,1,0:T(8,128)(2,1)} %bitcast.57), custom_call_target="tpu_custom_call" | custom-call | flops 20000000000 | bytes 6000000 | tf_op jit(solution)/shard_map/attention/pallas_call | solution.py:135
  91.6 1.9 collective-permute-start.1
  93.5 0.1 iota_compare_fusion.1
  93.6 13.9 %collective-permute-done.1 = bf16[512,192]{1,0:T(8,128)(2,1)S(1)} collective-permute-done((bf16[512,192]{1,0:T(8,128)(2,1)S(1)}, bf16[512,192]{1,0:T(8,128)(2,1)S(1)}, u32[]{:S(2)}, u32[]{:S(2)}) %collective-permute-start.1) | collective-permute-done | bytes 196640 | tf_op jit(solution)/shard_map/ppermute | solution.py:154
  107.5 0.1 pad_maximum_fusion.1
  107.6 0.0 copy-start.2
  107.6 1.0 copy.21
  108.6 6.3 %all-to-all-start = ((bf16[8,128,192]{1,2,0:T(8,128)(2,1)}), bf16[8,128,192]{1,2,0:T(8,128)(2,1)S(1)}, u32[]{:S(2)}, u32[]{:S(2)}) async-start(bf16[8,128,192]{1,2,0:T(8,128)(2,1)} %copy.21), calls=%async_computation | async-start | bytes 786432 | tf_op jit(solution)/shard_map/all_to_all | solution.py:456
  114.8 0.6 fusion.7.combine_ref
  115.5 0.0 copy-done
  115.5 1.3 convolution_convert_fusion
  116.8 8.4 %all-to-all-done = bf16[8,128,192]{1,2,0:T(8,128)(2,1)S(1)} async-done(((bf16[8,128,192]{1,2,0:T(8,128)(2,1)}), bf16[8,128,192]{1,2,0:T(8,128)(2,1)S(1)}, u32[]{:S(2)}, u32[]{:S(2)}) %all-to-all-start) | async-done | bytes 393248 | tf_op jit(solution)/shard_map/all_to_all | solution.py:456
  125.2 0.0 copy-done.2
  125.2 4.6 %fusion.1 = (f32[128]{0:T(128)S(1)}, bf16[128,2560]{1,0:T(8,128)(2,1)S(1)}) fusion(bf16[128,1536]{0,1:T(8,128)(2,1)S(1)} %bitcast.45, bf16[1536,2560]{1,0:T(8,128)(2,1)} %param.14, bf16[128,2560]{1,0:T(8,128)(2,1)S(1)} %copy-done.2), kind=kOutput, calls=%fused_computation.8 | convolution fusion | flops 1008598912 | bytes 9568768 | tf_op jit(solution)/shard_map/dot_general | solution.py:457
  129.7 0.0 copy-start.1
  129.7 1.3 convolution_convert_fusion.1
  131.0 0.0 all-gather.11.cloned.1.call-done
  131.0 0.0 all-gather.13.cloned.1.call-done
  131.0 10.2 %all-gather.15.cloned.1.call-done = bf16[1,512,2560]{2,1,0:T(8,128)(2,1)} async-done(((bf16[1,64,2560]{2,1,0:T(8,128)(2,1)}), bf16[1,512,2560]{2,1,0:T(8,128)(2,1)}) %all-gather.15.cloned.1.call-update) | async-done | bytes 2621456 | tf_op jit(solution)/shard_map/all_gather | solution.py:455
  141.2 0.0 copy-done.1
  141.2 84.6 %experts.1 = (bf16[128,2560]{1,0:T(8,128)(2,1)}, bf16[1,64,2560]{2,1,0:T(8,128)(2,1)}, bf16[1,64,2560]{2,1,0:T(8,128)(2,1)}, bf16[1,64,2560]{2,1,0:T(8,128)(2,1)}) custom-call(bf16[8,16,2560]{2,1,0:T(8,128)(2,1)} %bitcast.54, bf16[8,16,2560]{2,1,0:T(8,128)(2,1)} %bitcast.53, bf16[512,2560]{1,0:T(8,128)(2,1)} %bitcast.58, bf16[512,2560]{1,0:T(8,128)(2,1)} %bitcast.59, ...), custom_call_target="tpu_custom_call" | custom-call | flops 5000000000 | bytes 20000000 | tf_op jit(solution)/shard_map/experts/pallas_call | solution.py:386
  225.8 0.0 copy-start.6
  225.8 0.0 copy-start.5
  225.8 2.0 copy.28
  227.9 1.7 copy.29
  229.6 0.0 copy-done.6
  229.6 0.7 copy.30
  230.3 0.0 copy-done.5
  230.3 0.7 copy.31
  (10 shorter events, 0.2 us)
Async XLA Ops:
  7.2 108.3 %copy-start = (bf16[128,2560]{1,0:T(8,128)(2,1)S(1)}, bf16[128,2560]{1,0:T(8,128)(2,1)}, u32[]{:S(2)}) copy-start(bf16[128,2560]{1,0:T(8,128)(2,1)} %param.21) | copy-start | bytes 1966084
  7.2 4.8 %copy-start.4 = (bf16[1024,192]{0,1:T(8,128)(2,1)S(1)}, bf16[1024,192]{0,1:T(8,128)(2,1)}, u32[]{:S(2)}) copy-start(bf16[1024,192]{0,1:T(8,128)(2,1)} %param.12) | copy-start | bytes 1179652
  7.2 44.4 %all-gather.9.cloned.1.call-start = ((), (), s32[]{:S(2)}) async-start(), calls=%async_computation.1 | async-start | bytes 4456448 | tf_op jit(solution)/shard_map/all_gather | solution.py:121
  10.4 120.6 %all-gather.11.cloned.1.call-start = ((), (), s32[]{:S(2)}) async-start(), calls=%async_computation.2 | async-start | bytes 2949120 | tf_op jit(solution)/shard_map/all_gather | solution.py:455
  11.2 119.9 %all-gather.13.cloned.1.call-start = ((), (), s32[]{:S(2)}) async-start(), calls=%async_computation.3 | async-start | bytes 2949120 | tf_op jit(solution)/shard_map/all_gather | solution.py:455
  11.9 6.0 %copy-start.8 = (s32[128]{0:T(128)S(1)}, s32[128]{0:T(128)}, u32[]{:S(2)}) copy-start(s32[128]{0:T(128)} %param.16) | copy-start | bytes 1540
  11.9 6.0 %copy-start.3 = (s32[128256]{0:T(1024)S(1)}, s32[128256]{0:T(1024)}, u32[]{:S(2)}) copy-start(s32[128256]{0:T(1024)} %param.17) | copy-start | bytes 1539076
  11.9 129.3 %all-gather.15.cloned.1.call-start = ((), (), s32[]{:S(2)}) async-start(), calls=%async_computation.4 | async-start | bytes 2949120 | tf_op jit(solution)/shard_map/all_gather | solution.py:455
  12.0 7.6 %copy-start.7 = (bf16[2560]{0:T(1024)(128)(2,1)S(1)}, bf16[2560]{0:T(1024)(128)(2,1)}, u32[]{:S(2)}) copy-start(bf16[2560]{0:T(1024)(128)(2,1)} %param.15) | copy-start | bytes 15364
  12.0 10.3 %collective-permute-start = (bf16[512,192]{0,1:T(8,128)(2,1)S(1)}, bf16[512,192]{0,1:T(8,128)(2,1)S(1)}, u32[]{:S(2)}, u32[]{:S(2)}) collective-permute-start(bf16[512,192]{0,1:T(8,128)(2,1)S(1)} %get-tuple-element.7), channel_id=1, source_target_pairs={{0,120},{8,112},{16,104},{24,96},{32,88},{40,80},{48,72},{56,64},{... | collective-permute-start | bytes 589832 | tf_op jit(solution)/shard_map/ppermute | solution.py:122
  91.6 15.9 %collective-permute-start.1 = (bf16[512,192]{1,0:T(8,128)(2,1)S(1)}, bf16[512,192]{1,0:T(8,128)(2,1)S(1)}, u32[]{:S(2)}, u32[]{:S(2)}) collective-permute-start(bf16[512,192]{1,0:T(8,128)(2,1)S(1)} %get-tuple-element.5), channel_id=1, source_target_pairs={{0,120},{8,112},{16,104},{24,96},{32,88},{40,80},{48,72},{56,64},{... | collective-permute-start | bytes 589832 | tf_op jit(solution)/shard_map/ppermute | solution.py:154
  107.6 17.6 %copy-start.2 = (bf16[128,2560]{1,0:T(8,128)(2,1)S(1)}, bf16[128,2560]{1,0:T(8,128)(2,1)}, u32[]{:S(2)}) copy-start(bf16[128,2560]{1,0:T(8,128)(2,1)} %param.11) | copy-start | bytes 1966084
  108.6 16.6 %all-to-all-start = ((bf16[8,128,192]{1,2,0:T(8,128)(2,1)}), bf16[8,128,192]{1,2,0:T(8,128)(2,1)S(1)}, u32[]{:S(2)}, u32[]{:S(2)}) async-start(bf16[8,128,192]{1,2,0:T(8,128)(2,1)} %copy.21), calls=%async_computation | async-start | bytes 786432 | tf_op jit(solution)/shard_map/all_to_all | solution.py:456
  129.7 11.5 %copy-start.1 = (bf16[128,2560]{1,0:T(8,128)(2,1)}, bf16[128,2560]{1,0:T(8,128)(2,1)S(1)}, u32[]{:S(2)}) copy-start(bf16[128,2560]{1,0:T(8,128)(2,1)S(1)} %get-tuple-element.15.hidden_ref) | copy-start | bytes 1966084
  225.8 3.8 %copy-start.6 = (bf16[1,64,2560]{2,1,0:T(8,128)(2,1)S(1)}, bf16[1,64,2560]{2,1,0:T(8,128)(2,1)}, u32[]{:S(2)}) copy-start(bf16[1,64,2560]{2,1,0:T(8,128)(2,1)} %get-tuple-element.24) | copy-start | bytes 983044
  225.8 4.5 %copy-start.5 = (bf16[1,64,2560]{2,1,0:T(8,128)(2,1)S(1)}, bf16[1,64,2560]{2,1,0:T(8,128)(2,1)}, u32[]{:S(2)}) copy-start(bf16[1,64,2560]{2,1,0:T(8,128)(2,1)} %get-tuple-element.25) | copy-start | bytes 983044
Sparse Core Ops, SparseCore 0:
  10.5 41.0 all-gather.8
  53.3 26.1 all-gather.10
  81.2 31.7 all-gather.12
  114.6 26.5 all-gather.14

commit v3 on v2

--- a/solution.py
+++ b/solution.py
@@ -11,7 +11,6 @@
 
 HEAD_DIM = 64
 SEQ = ("zl", "y", "c")
-UNITS = ("c", "y")
 MESH = pl.DeviceIdType.MESH
 score_to_log2 = math.log2(math.e) / math.sqrt(HEAD_DIM)
 very_negative = -1e30
@@ -46,26 +45,215 @@
     return (gate_grad, up_grad)
 
 
-def attention_kernel(place, q_ref, kv_ref, out_ref, m_ref, acc_ref):
-    half_rows = out_ref.shape[1]
-    heads = out_ref.shape[2] // HEAD_DIM
-    shard_rows = 2 * half_rows
+def neighbour(**place):
+    return {axis: place.get(axis, lax.axis_index(axis)) for axis in (*SEQ, "exp")}
+
+
+ARRIVALS = (
+    (0, 0, 0),
+    (0, 0, 1),
+    (1, 0, 0),
+    (0, 3, 0),
+    (0, 1, 0),
+    (1, 1, 0),
+    (1, 3, 0),
+    (0, 2, 0),
+    (1, 2, 0),
+    (1, 0, 1),
+    (0, 3, 1),
+    (0, 1, 1),
+    (1, 1, 1),
+    (1, 3, 1),
+    (0, 2, 1),
+    (1, 2, 1),
+)
+WEIGHTS_START = 1
+WEIGHTS_PASS = 13
+
+
+def attention_kernel(
+    queries_ref,
+    keyvals_ref,
+    grads_ref,
+    gate_ref,
+    up_ref,
+    down_ref,
+    heads_out,
+    grads_out,
+    weights_out,
+    kv_all,
+    odd_in,
+    turned,
+    m_ref,
+    acc_ref,
+    mixed_ref,
+    kv_send,
+    kv_recv,
+    odd_sem,
+    push_send,
+    push_recv,
+    heads_send,
+    heads_recv,
+    weight_send,
+    weight_recv,
+    local_sem,
+):
+    zl, y, c, ex = (lax.axis_index(a) for a in (*SEQ, "exp"))
+    half_rows = odd_in.shape[0]
+    heads = odd_in.shape[1] // HEAD_DIM
     pieces = half_rows // 128
+    experts = grads_ref.shape[0]
+    shard = zl * 8 + y * 2 + c
+    mirror = 15 - shard
+    core_peer = neighbour(c=1 - c)
+    z_peer = neighbour(zl=1 - zl)
+    y_up = neighbour(y=lax.rem(y + 1, 4))
+    y_down = neighbour(y=lax.rem(y + 3, 4))
+
+    def mirrored(e):
+        return {"zl": 1 - zl, "y": 3 - y, "c": 1 - c, "exp": e}
+
+    barrier = pltpu.get_barrier_semaphore()
+    greeted = [core_peer, y_up, y_down]
+    for d in range(experts):
+        e = lax.rem(ex + d, experts)
+        greeted += [mirrored(e), neighbour(zl=1 - zl, exp=e)]
+        if d:
+            greeted.append(neighbour(exp=e))
+    for other in greeted:
+        pl.semaphore_signal(barrier, inc=1, device_id=other, device_id_type=MESH)
+
+    own_weights = [
+        pltpu.make_async_copy(ref.at[0], weights_out.at[n, c, y], local_sem.at[n])
+        for n, ref in enumerate((gate_ref, up_ref, down_ref))
+    ]
+    own_grads = pltpu.make_async_copy(grads_ref.at[ex], grads_out.at[zl, ex], local_sem.at[3])
+    for copy in (*own_weights, own_grads):
+        copy.start()
+
+    keyvals = keyvals_ref[...]
+    kv_all[shard, pl.ds(0, half_rows), :] = jnp.concatenate(
+        [keyvals[:half_rows, :HEAD_DIM], keyvals[half_rows:, :HEAD_DIM]], axis=1
+    )
+    values = keyvals.T[HEAD_DIM:]
+    for p in range(2 * pieces):
+        kv_all[shard, pl.ds(half_rows + p * HEAD_DIM, HEAD_DIM), :] = values[
+            :, p * 128 : (p + 1) * 128
+        ]
+
+    def turn(half, rows):
+        flipped = rows.T
+        flat = jnp.concatenate(
+            [flipped[h * HEAD_DIM : (h + 1) * HEAD_DIM] for h in range(heads)], axis=1
+        )
+        empty = jnp.zeros_like(flat)
+        turned[half, 0] = jnp.concatenate([flat, empty], axis=0)
+        turned[half, 1] = jnp.concatenate([empty, flat], axis=0)
+
+    turn(0, queries_ref[pl.ds(0, half_rows), :])
+    m_ref[...] = jnp.full_like(m_ref, very_negative)
+    acc_ref[...] = jnp.zeros_like(acc_ref)
+    pl.semaphore_wait(barrier, len(greeted))
+
+    odd_copy = pltpu.make_async_remote_copy(
+        src_ref=queries_ref.at[pl.ds(half_rows, half_rows)],
+        dst_ref=odd_in,
+        send_sem=odd_sem.at[0],
+        recv_sem=odd_sem.at[1],
+        device_id=mirrored(ex),
+        device_id_type=MESH,
+    )
+
+    def shard_at(dz, dy, dc):
+        return lax.rem(zl + dz, 2) * 8 + lax.rem(y + dy, 4) * 2 + lax.rem(c + dc, 2)
+
+    def pass_on(index, t, to):
+        return pltpu.make_async_remote_copy(
+            src_ref=kv_all.at[t],
+            dst_ref=kv_all.at[t],
+            send_sem=kv_send.at[index],
+            recv_sem=kv_recv.at[t],
+            device_id=to,
+            device_id_type=MESH,
+        )
+
+    routes = {
+        (0, 0, 0): (z_peer, y_up, y_down, core_peer),
+        (1, 0, 0): (y_up, y_down, core_peer),
+        (0, 3, 0): (y_up, core_peer),
+        (0, 1, 0): (core_peer,),
+        (1, 1, 0): (y_down, core_peer),
+        (1, 3, 0): (core_peer,),
+        (0, 2, 0): (core_peer,),
+        (1, 2, 0): (core_peer,),
+    }
+    forwards = {}
+    for place, targets in routes.items():
+        first = sum(len(f) for f in forwards.values())
+        forwards[place] = [
+            pass_on(first + n, shard_at(*place), to) for n, to in enumerate(targets)
+        ]
+
+    def weight_copy(index, rows, dy, to, dc=0):
+        part = weights_out.at[:, lax.rem(c + dc, 2), lax.rem(y + dy, 4), rows]
+        return pltpu.make_async_remote_copy(
+            src_ref=part,
+            dst_ref=part,
+            send_sem=weight_send.at[index],
+            recv_sem=weight_recv.at[index],
+            device_id=to,
+            device_id_type=MESH,
+        )
+
+    owned = weights_out.shape[3]
+    every, low, high = pl.ds(0, owned), pl.ds(0, owned // 2), pl.ds(owned // 2, owned // 2)
+    weight_own = [
+        weight_copy(0, every, 0, y_up),
+        weight_copy(1, every, 0, y_down),
+        weight_copy(2, every, 0, core_peer),
+    ]
+    weight_above = weight_copy(3, low, 3, y_up)
+    weight_below = weight_copy(4, high, 1, y_down)
+    weight_core = [
+        weight_copy(5, every, 3, core_peer),
+        weight_copy(6, every, 1, core_peer),
+        weight_copy(7, every, 2, core_peer),
+    ]
+
+    pushes = []
+    for index in range(1, 2 * experts):
+        dz, de = divmod(index, experts)
+        e = lax.rem(ex + de, experts)
+        pushes.append(
+            pltpu.make_async_remote_copy(
+                src_ref=grads_ref.at[e],
+                dst_ref=grads_out.at[zl, ex],
+                send_sem=push_send.at[index],
+                recv_sem=push_recv.at[index],
+                device_id=neighbour(zl=lax.rem(zl + dz, 2), exp=e),
+                device_id_type=MESH,
+            )
+        )
+
+    for copy in forwards[(0, 0, 0)]:
+        copy.start()
+    odd_copy.start()
+
     ones = jnp.ones((16, half_rows), jnp.bfloat16)
 
     def values_of(block, part):
-        turned = [
-            kv_ref[block, pl.ds(half_rows + (part * pieces + j) * HEAD_DIM, HEAD_DIM), :]
-            for j in range(pieces)
+        turned_values = [
+            kv_all[block, pl.ds(half_rows + (part * pieces + p) * HEAD_DIM, HEAD_DIM), :]
+            for p in range(pieces)
         ]
-        return jnp.concatenate([jnp.concatenate(turned, axis=1), ones], axis=0)
+        return jnp.concatenate([jnp.concatenate(turned_values, axis=1), ones], axis=0)
 
     def step(half, block, parts, masked):
-        keys = kv_ref[block, pl.ds(0, half_rows), :]
+        keys = kv_all[block, pl.ds(0, half_rows), :]
         scores = []
         for part in range(parts):
             s = (
-                jnp.dot(keys, q_ref[half, part], preferred_element_type=jnp.float32)
+                jnp.dot(keys, turned[half, part], preferred_element_type=jnp.float32)
                 * score_to_log2
             )
             if masked and part == parts - 1:
@@ -73,98 +261,205 @@
                 query_place = lax.broadcasted_iota(jnp.int32, s.shape, 1) % half_rows
                 s = jnp.where(key_place <= query_place, s, very_negative)
             scores.append(s)
-        old = m_ref[...]
+        old = m_ref[half]
         new = old
         for s in scores:
             new = jnp.maximum(new, jnp.max(s, axis=0, keepdims=True))
-        m_ref[...] = new
-        total = acc_ref[...] * jnp.exp2(old - new)
+        m_ref[half] = new
+        total = acc_ref[half] * jnp.exp2(old - new)
         for part, s in enumerate(scores):
             weights = jnp.exp2(s - new).astype(jnp.bfloat16)
             total += jnp.dot(values_of(block, part), weights, preferred_element_type=jnp.float32)
-        acc_ref[...] = total
-
-    def run(half, full_blocks, last_parts):
-        m_ref[...] = jnp.full_like(m_ref, very_negative)
-        acc_ref[...] = jnp.zeros_like(acc_ref)
-
-        def body(block, carry):
-            step(half, block, 2, False)
-            return carry
-
-        lax.fori_loop(0, full_blocks, body, 0)
-        step(half, full_blocks, last_parts, True)
-        mixed = acc_ref[pl.ds(0, HEAD_DIM), :] / acc_ref[pl.ds(HEAD_DIM, 1), :]
+        acc_ref[half] = total
+
+    step(0, shard, 1, True)
+    odd_copy.wait_recv()
+    turn(1, odd_in[...])
+
+    def visit(slot, carry):
+        def pick(axis):
+            return sum(
+                jnp.where(slot == n, place[axis], 0) for n, place in enumerate(ARRIVALS)
+            )
+
+        t = shard_at(pick(0), pick(1), pick(2))
+
+        @pl.when(slot > 0)
+        def _():
+            pass_on(0, t, core_peer).wait_recv()
+
+        for n, place in enumerate(ARRIVALS):
+            if n and place in forwards:
+
+                @pl.when(slot == n)
+                def _():
+                    for copy in forwards[place]:
+                        copy.start()
+
+        @pl.when(slot == WEIGHTS_START)
+        def _():
+            for copy in own_weights:
+                copy.wait()
+            for copy in (*weight_own, *pushes):
+                copy.start()
+
+        @pl.when(slot == WEIGHTS_PASS)
+        def _():
+            weight_own[0].wait_recv()
+            weight_above.start()
+            weight_core[0].start()
+            weight_own[1].wait_recv()
+            weight_below.start()
+            weight_core[1].start()
+
+        def one_half(half, inner):
+            @pl.when(t < jnp.where(half == 0, shard, mirror))
+            def _():
+                step(half, t, 2, False)
+
+            return inner
+
+        lax.fori_loop(0, 2, one_half, 0)
+        return carry
+
+    lax.fori_loop(0, len(ARRIVALS), visit, 0)
+    step(1, mirror, 2, True)
+
+    for half in range(2):
+        total = acc_ref[half]
+        mixed = total[:HEAD_DIM] / total[HEAD_DIM : HEAD_DIM + 1]
         for head in range(heads):
-            out_ref[half, :, pl.ds(head * HEAD_DIM, HEAD_DIM)] = (
+            mixed_ref[half, :, pl.ds(head * HEAD_DIM, HEAD_DIM)] = (
                 mixed[:, head * half_rows : (head + 1) * half_rows].T.astype(jnp.bfloat16)
             )
 
-    shard = place[0]
-    mirror = place[1]
-    run(1, mirror, 2)
-    run(0, shard, 1)
-
-
-def attend(queries, keyvals):
-    row_count = queries.shape[0]
+    def head_copy(half, block, to):
+        return pltpu.make_async_remote_copy(
+            src_ref=mixed_ref.at[half, pl.ds(pl.multiple_of(block * 128, 128), 128)],
+            dst_ref=heads_out.at[ex],
+            send_sem=heads_send.at[half, block],
+            recv_sem=heads_recv.at[ex],
+            device_id=to,
+            device_id_type=MESH,
+        )
+
+    even_copies = []
+    for d in range(4):
+        block = lax.rem(ex + d, 4)
+        even_copies.append(head_copy(0, block, neighbour(exp=block)))
+    odd_copies = []
+    for d in range(4):
+        block = lax.rem(ex + d, 4)
+        odd_copies.append(head_copy(1, block, mirrored(4 + block)))
+    own_heads = pltpu.make_async_copy(
+        mixed_ref.at[0, pl.ds(pl.multiple_of(lax.rem(ex, 4) * 128, 128), 128)],
+        heads_out.at[ex],
+        local_sem.at[4],
+    )
+    for copy in (*odd_copies, *even_copies[1:]):
+        copy.start()
+
+    @pl.when(ex < 4)
+    def _():
+        own_heads.start()
+
+    @pl.when(ex >= 4)
+    def _():
+        even_copies[0].start()
+
+    weight_above.wait_recv()
+    weight_below.wait_recv()
+    weight_core[2].start()
+
+    def head_arrival(e):
+        return pltpu.make_async_remote_copy(
+            src_ref=mixed_ref.at[0, pl.ds(0, 128)],
+            dst_ref=heads_out.at[e],
+            send_sem=heads_send.at[0, 0],
+            recv_sem=heads_recv.at[e],
+            device_id=core_peer,
+            device_id_type=MESH,
+        )
+
+    for d in range(1, experts):
+        head_arrival(lax.rem(ex + d, experts)).wait_recv()
+
+    @pl.when(ex < 4)
+    def _():
+        own_heads.wait()
+
+    @pl.when(ex >= 4)
+    def _():
+        head_arrival(ex).wait_recv()
+        even_copies[0].wait_send()
+
+    own_grads.wait()
+    for copy in pushes:
+        copy.wait()
+    weight_own[2].wait_recv()
+    for copy in weight_core:
+        copy.wait_recv()
+    odd_copy.wait_send()
+    for copies in forwards.values():
+        for copy in copies:
+            copy.wait_send()
+    for copy in (*weight_own, weight_above, weight_below, *weight_core):
+        copy.wait_send()
+    for copy in (*odd_copies, *even_copies[1:]):
+        copy.wait_send()
+
+
+def attend(queries, keyvals, send_grads, w_gate, w_up, w_down):
+    row_count, query_width = queries.shape
     half_rows = row_count // 2
-    heads = queries.shape[1] // HEAD_DIM
-    shard_count = lax.axis_size(SEQ)
-    shard = lax.axis_index(SEQ)
-    swap = [(s, shard_count - 1 - s) for s in range(shard_count)]
-    keys = keyvals[:, :HEAD_DIM]
-    keys = jnp.concatenate([keys[:half_rows], keys[half_rows:]], axis=1)
-    values = keyvals[:, HEAD_DIM:].reshape(row_count // 128, 128, HEAD_DIM)
-    values = jnp.transpose(values, (0, 2, 1)).reshape(half_rows, 2 * HEAD_DIM)
-    packed = jnp.concatenate([keys, values], axis=0)
-    gathered = lax.all_gather(packed, SEQ, axis=0, tiled=False)
-    odd = lax.ppermute(queries[half_rows:], SEQ, swap)
-
-    def turn(rows):
-        turned = jnp.transpose(rows.reshape(half_rows, heads, HEAD_DIM), (2, 1, 0)).reshape(
-            HEAD_DIM, heads * half_rows
-        )
-        empty = jnp.zeros_like(turned)
-        return jnp.stack(
-            [jnp.concatenate([turned, empty], axis=0), jnp.concatenate([empty, turned], axis=0)]
-        )
-
-    turned_queries = jnp.stack([turn(queries[:half_rows]), turn(odd)])
-    place = jnp.stack([shard, shard_count - 1 - shard]).astype(jnp.int32)
-    mixed = pl.pallas_call(
+    heads = query_width // HEAD_DIM
+    experts, capacity, width = send_grads.shape
+    owned = w_gate.shape[1]
+    bf16 = jnp.bfloat16
+    vmem = pl.BlockSpec(memory_space=pltpu.VMEM)
+    anywhere = pl.BlockSpec(memory_space=pl.ANY)
+    dma = pltpu.SemaphoreType.DMA
+    return pl.pallas_call(
         attention_kernel,
-        out_shape=jax.ShapeDtypeStruct((2, half_rows, heads * HEAD_DIM), jnp.bfloat16),
-        in_specs=[
-            pl.BlockSpec(memory_space=pltpu.SMEM),
-            pl.BlockSpec(memory_space=pltpu.VMEM),
-            pl.BlockSpec(memory_space=pltpu.VMEM),
+        out_shape=(
+            jax.ShapeDtypeStruct((experts, row_count // experts, query_width), bf16),
+            jax.ShapeDtypeStruct((2, experts, capacity, width), bf16),
+            jax.ShapeDtypeStruct((3, 2, 4, owned, width), bf16),
+        ),
+        in_specs=[vmem] * 2 + [anywhere] * 4,
+        out_specs=(anywhere,) * 3,
+        scratch_shapes=[
+            pltpu.VMEM((len(ARRIVALS), row_count, 2 * HEAD_DIM), bf16),
+            pltpu.VMEM((half_rows, query_width), bf16),
+            pltpu.VMEM((2, 2, 2 * HEAD_DIM, heads * half_rows), bf16),
+            pltpu.VMEM((2, 1, heads * half_rows), jnp.float32),
+            pltpu.VMEM((2, HEAD_DIM + 16, heads * half_rows), jnp.float32),
+            pltpu.VMEM((2, half_rows, query_width), bf16),
+            dma((15,)),
+            dma((len(ARRIVALS),)),
+            dma((2,)),
+            dma((2 * experts,)),
+            dma((2 * experts,)),
+            dma((2, 4)),
+            dma((experts,)),
+            dma((8,)),
+            dma((8,)),
+            dma((5,)),
         ],
-        out_specs=pl.BlockSpec(memory_space=pltpu.VMEM),
-        scratch_shapes=[
-            pltpu.VMEM((1, heads * half_rows), jnp.float32),
-            pltpu.VMEM((HEAD_DIM + 16, heads * half_rows), jnp.float32),
-        ],
-        compiler_params=pltpu.CompilerParams(vmem_limit_bytes=48 * 2**20),
+        compiler_params=pltpu.CompilerParams(
+            collective_id=0, has_side_effects=True, vmem_limit_bytes=48 * 2**20
+        ),
         cost_estimate=pl.CostEstimate(
-            flops=20_000_000_000, bytes_accessed=6_000_000, transcendentals=27_000_000
+            flops=20_000_000_000, bytes_accessed=20_000_000, transcendentals=27_000_000
         ),
         name="attention",
-    )(place, turned_queries, gathered)
-    back = lax.ppermute(mixed[1], SEQ, swap)
-    return jnp.concatenate([mixed[0], back], axis=0)
-
-
-def neighbour(**place):
-    return {axis: place.get(axis, lax.axis_index(axis)) for axis in (*SEQ, "exp")}
+    )(queries, keyvals, send_grads, w_gate, w_up, w_down)
 
 
 def expert_kernel(
     rows_ref,
-    cot_ref,
-    gate_ref,
-    up_ref,
-    down_ref,
+    cot_in,
+    weights_ref,
     hidden_ref,
     combine_ref,
     layer_ref,
@@ -172,7 +467,6 @@
     grad_up_ref,
     grad_down_ref,
     rows_in,
-    cot_in,
     out_buf,
     out_in,
     parts,
@@ -243,7 +537,6 @@
         for copy in sent:
             copy.wait_recv()
 
-    cot_copies = spread(0, cot_ref, cot_in)
     rows_copies = spread(1, rows_ref, rows_in)
 
     def flat(ref):
@@ -316,13 +609,13 @@
             jnp.bfloat16
         )
 
-    arrive(cot_copies)
+    gate, up, down = (weights_ref[n].reshape(-1, width) for n in range(3))
     output_grads = flat(cot_in)
-    hidden_grad = contract_cols(output_grads, down_ref[...])
+    hidden_grad = contract_cols(output_grads, down)
     arrive(rows_copies)
     expert_rows = flat(rows_in)
-    gate_act = contract_cols(expert_rows, gate_ref[...])
-    up_act = contract_cols(expert_rows, up_ref[...])
+    gate_act = contract_cols(expert_rows, gate)
+    up_act = contract_cols(expert_rows, up)
     hidden_units = swiglu_forward(gate_act, up_act)
     partial(0, hidden_units, output_grads)
     core_down = core_stage(0)
@@ -337,7 +630,7 @@
         out_buf[:, :, :, pl.ds(start, chunk)] = (
             jnp.dot(
                 hidden_units,
-                down_ref[:, pl.ds(start, chunk)],
+                down[:, start : start + chunk],
                 preferred_element_type=jnp.float32,
             )
             .astype(jnp.bfloat16)
@@ -369,14 +662,13 @@
         ).astype(jnp.bfloat16)
     finish(1, full_gate, grad_gate_ref)
     finish(2, full_up, grad_up_ref)
-    for copy in (*cot_copies[1], *rows_copies[1], *back, *started):
+    for copy in (*rows_copies[1], *back, *started):
         copy.wait_send()
 
 
-def expert_layer(send_rows, send_grads, weights, hidden_state, dispatch_table):
+def expert_layer(send_rows, grad_rows, weights, hidden_state, dispatch_table):
     experts, capacity, width = send_rows.shape
-    units = weights[0].shape[0]
-    owned = units // 8
+    owned = weights.shape[3]
     token_count = hidden_state.shape[0]
     combine = jnp.concatenate([dispatch_table, dispatch_table], axis=0).T
     vmem = pl.BlockSpec(memory_space=pltpu.VMEM)
@@ -386,10 +678,9 @@
     return pl.pallas_call(
         expert_kernel,
         out_shape=(jax.ShapeDtypeStruct((token_count, width), bf16),) + (grad_shape,) * 3,
-        in_specs=[vmem] * 7,
+        in_specs=[vmem] * 5,
         out_specs=(vmem,) * 4,
         scratch_shapes=[
-            landing,
             landing,
             landing,
             landing,
@@ -413,7 +704,7 @@
             flops=5_000_000_000, bytes_accessed=20_000_000, transcendentals=200_000
         ),
         name="experts",
-    )(send_rows, send_grads, *weights, hidden_state, combine)
+    )(send_rows, grad_rows, weights, hidden_state, combine)
 
 
 def local(
@@ -451,17 +742,21 @@
             .reshape(expert_count, capacity, model_width)
         )
 
-    attention = attend(queries, keyvals)
-    weights = [lax.all_gather(w[0], UNITS, axis=0, tiled=True) for w in (w_gate, w_up, w_down)]
-    token_heads = lax.all_to_all(attention, "exp", split_axis=0, concat_axis=1, tiled=True)
-    projected = jnp.dot(token_heads, out_proj, preferred_element_type=jnp.float32)
+    token_heads, grad_rows, weights = attend(
+        queries, keyvals, placed(cotangent), w_gate, w_up, w_down
+    )
+    projected = jnp.dot(
+        jnp.transpose(token_heads, (1, 0, 2)).reshape(token_count, -1),
+        out_proj,
+        preferred_element_type=jnp.float32,
+    )
     hidden_state = (resid.astype(jnp.float32) + projected).astype(jnp.bfloat16)
     widened = hidden_state.astype(jnp.float32)
     mean_square = jnp.mean(widened * widened, axis=1, keepdims=True)
     normed = (widened * lax.rsqrt(mean_square + norm_eps) * norm_gain.astype(jnp.float32)).astype(
         jnp.bfloat16
     )
-    return expert_layer(placed(normed), placed(cotangent), weights, hidden_state, dispatch_table)
+    return expert_layer(placed(normed), grad_rows, weights, hidden_state, dispatch_table)
 
 
 def solution(mesh):

time: 238 us -> 186 us (0.78)
  waiting for transfers between devices: 65.2 us -> 0 us
  Pallas kernels: 125 us -> 165 us
  starting transfers between devices: 13.9 us -> 0 us
  between operations: 14.1 us -> 0.81 us
    pallas_call x1, Pallas kernels: 39.9 us -> 97 us  [attend(): pl.pallas_call(attention_kernel, out_shape=(jax.ShapeDtypeStruct((experts...]
    all_gather x4 -> x0, waiting for transfers between devices: 38.9 us -> none  [the longest x1 28.7 us: attend(): gathered = lax.all_gather(packed, SEQ, axis=0, tiled=False)]
    ppermute x2 -> x0, waiting for transfers between devices: 16.5 us -> none  [the longest x1 13.9 us: attend(): back = lax.ppermute(mixed[1], SEQ, swap)]
    pallas_call x1, Pallas kernels: 84.6 us -> 68.3 us  [expert_layer(): pl.pallas_call(expert_kernel, out_shape=(jax.ShapeDtypeStruct((token_coun...]
    all_to_all x1 -> x0, waiting for transfers between devices: 8.38 us -> none  [local(): lax.all_to_all(attention, 'exp', split_axis=0, concat_axis=1, tiled=True)]
    ppermute x2 -> x0, starting transfers between devices: 7.47 us -> none  [the longest x1 5.56 us: attend(): odd = lax.ppermute(queries[half_rows:], SEQ, swap)]
    all_to_all x1 -> x0, starting transfers between devices: 6.27 us -> none  [local(): lax.all_to_all(attention, 'exp', split_axis=0, concat_axis=1, tiled=True)]
    unnamed x24 -> x27, local copies, waits for them, and re-layouts: 5.34 us -> 7.44 us
  transfers between devices with their start and end apart: 7 -> 0, of which waited for: 5 -> 0; matrix products, arithmetic and copies ran while one was open for 5% -> 0% of each run, Pallas kernels for 17% -> 0%
where the time goes in v3:
time: 186 us; the launch traced here: 185 us
  Pallas kernels  165 us (89%)
  local copies, waits for them, and re-layouts  9.66 us (5%)
  matrix products  6.28 us (3%)
  other arithmetic  3.35 us (2%)
    pallas_call x1, Pallas kernels, attend(): pl.pallas_call(attention_kernel, out_shape=(jax.ShapeDtypeStruct((experts...  97 us
    pallas_call x1, Pallas kernels, expert_layer(): pl.pallas_call(expert_kernel, out_shape=(jax.ShapeDtypeStruct((token_coun...  68.3 us
    unnamed x27, local copies, waits for them, and re-layouts  7.44 us
    dot_general x1, matrix products, local(): jnp.dot(jnp.transpose(token_heads, (1, 0, 2)).reshape(token_count, -1), o...  4.55 us

profile of v3, /device:TPU:1, one launch (start us, length us, event | category | flops | bytes accessed | tf_op | source)
XLA Modules:
  0.0 185.4 jit_solution(6639112753579412928)
XLA Ops:
  0.6 0.0 copy-start
  0.6 0.7 compare_select_fusion
  1.4 2.0 %gather_fusion = s32[128]{0:T(128)S(1)} fusion(s32[128256]{0:T(1024)} %param.17, s32[1024]{0:T(1024)S(1)} %pad_clamp_fusion), kind=kCustom, calls=%fused_computation | custom fusion | bytes 1536 | tf_op jit(solution)/shard_map/jit(_take)/gather | solution.py:727
  3.3 0.0 copy-start.1
  3.3 0.0 copy-start.2
  3.4 0.0 copy-start.3
  3.4 0.0 copy-start.4
  3.4 0.8 and_select_fusion
  4.1 0.7 convert_element_type.30
  4.8 0.1 fusion.8
  4.9 0.2 reduce_window_sum.11
  5.1 0.2 select_reduce_fusion
  5.3 0.1 iota_compare_fusion.1
  5.4 0.6 fusion.7.combine_ref
  6.0 1.2 copy.16.queries_ref
  7.2 0.0 copy-done
  7.2 0.4 convolution_convert_fusion.1
  7.7 0.0 copy-done.1
  7.7 0.0 copy-done.2
  7.7 0.0 copy-done.3
  7.7 0.0 copy-done.4
  7.7 97.0 %attention.1 = (bf16[8,128,192]{2,1,0:T(8,128)(2,1)S(1)}, bf16[2,8,16,2560]{3,2,1,0:T(8,128)(2,1)S(1)}, bf16[3,2,4,64,2560]{4,3,2,1,0:T(8,128)(2,1)}) custom-call(bf16[1024,192]{1,0:T(8,128)(2,1)S(1)} %copy.16.queries_ref, bf16[1024,128]{1,0:T(8,128)(2,1)S(1)} %copy-done.4, bf16[8,16,2560]{2,1,0:T(8,128)(2,1)S(1)} %bitcast.9, ...), custom_call_target="tpu_custom_call" | custom-call | flops 20000000000 | bytes 20000000 | tf_op jit(solution)/shard_map/attention/pallas_call | solution.py:422
  104.8 0.0 copy-start.5
  104.8 1.1 copy-done.5
  105.9 0.0 copy-start.7
  105.9 0.3 copy.17
  106.2 0.8 copy-done.7
  107.0 4.5 %fusion.1 = (f32[128]{0:T(128)S(1)}, bf16[128,2560]{1,0:T(8,128)(2,1)S(1)}) fusion(bf16[128,1536]{0,1:T(8,128)(2,1)S(1)} %bitcast.11, bf16[1536,2560]{1,0:T(8,128)(2,1)} %param.14, bf16[128,2560]{1,0:T(8,128)(2,1)S(1)} %copy-done.7), kind=kOutput, calls=%fused_computation.7 | convolution fusion | flops 1008598912 | bytes 9568768 | tf_op jit(solution)/shard_map/dot_general | solution.py:748
  111.5 0.0 copy-start.6
  111.6 1.3 convolution_convert_fusion
  112.9 0.0 copy-done.6
  112.9 68.3 %experts.1 = (bf16[128,2560]{1,0:T(8,128)(2,1)}, bf16[1,64,2560]{2,1,0:T(8,128)(2,1)}, bf16[1,64,2560]{2,1,0:T(8,128)(2,1)}, bf16[1,64,2560]{2,1,0:T(8,128)(2,1)}) custom-call(bf16[8,16,2560]{2,1,0:T(8,128)(2,1)} %bitcast.12, bf16[2,8,16,2560]{3,2,1,0:T(8,128)(2,1)} %copy-done.5, bf16[3,2,4,64,2560]{4,3,2,1,0:T(8,128)(2,1)} %get-tuple-element.9.weights_ref, ...), custom_call_target="tpu_custom_call" | custom-call | flops 5000000000 | bytes 20000000 | tf_op jit(solution)/shard_map/experts/pallas_call | solution.py:678
  181.2 0.0 copy-start.10
  181.2 0.0 copy-start.9
  181.2 0.0 copy-start.8
  181.2 2.0 %copy.22 = bf16[128,2560]{1,0:T(8,128)(2,1)} copy(bf16[128,2560]{1,0:T(8,128)(2,1)} %get-tuple-element.16) | data formatting | bytes 1310720
  183.2 0.0 copy-done.10
  183.2 0.7 copy.23
  184.0 0.0 copy-done.9
  184.0 0.7 copy.24
  184.7 0.0 copy-done.8
  184.7 0.7 copy.25
  (3 shorter events, 0.0 us)
Async XLA Ops:
  0.6 6.6 %copy-start = (bf16[128,2560]{1,0:T(8,128)(2,1)S(1)}, bf16[128,2560]{1,0:T(8,128)(2,1)}, u32[]{:S(2)}) copy-start(bf16[128,2560]{1,0:T(8,128)(2,1)} %param.21) | copy-start | bytes 1966084
  3.3 4.3 %copy-start.1 = (bf16[1,64,2560]{2,1,0:T(8,128)(2,1)S(1)}, bf16[1,64,2560]{2,1,0:T(8,128)(2,1)}, u32[]{:S(2)}) copy-start(bf16[1,64,2560]{2,1,0:T(8,128)(2,1)} %gate_ref.1) | copy-start | bytes 983044
  3.3 4.3 %copy-start.2 = (bf16[1,64,2560]{2,1,0:T(8,128)(2,1)S(1)}, bf16[1,64,2560]{2,1,0:T(8,128)(2,1)}, u32[]{:S(2)}) copy-start(bf16[1,64,2560]{2,1,0:T(8,128)(2,1)} %up_ref.1) | copy-start | bytes 983044
  3.4 4.3 %copy-start.3 = (bf16[1,64,2560]{2,1,0:T(8,128)(2,1)S(1)}, bf16[1,64,2560]{2,1,0:T(8,128)(2,1)}, u32[]{:S(2)}) copy-start(bf16[1,64,2560]{2,1,0:T(8,128)(2,1)} %down_ref.1) | copy-start | bytes 983044
  3.4 4.3 %copy-start.4 = (bf16[1024,128]{1,0:T(8,128)(2,1)S(1)}, bf16[1024,128]{1,0:T(8,128)(2,1)}, u32[]{:S(2)}) copy-start(bf16[1024,128]{1,0:T(8,128)(2,1)} %keyvals_ref.1) | copy-start | bytes 786436
  104.8 1.2 copy-start.5
  105.9 1.1 copy-start.7
  111.5 1.3 copy-start.6
  181.2 2.1 %copy-start.10 = (bf16[1,64,2560]{2,1,0:T(8,128)(2,1)S(1)}, bf16[1,64,2560]{2,1,0:T(8,128)(2,1)}, u32[]{:S(2)}) copy-start(bf16[1,64,2560]{2,1,0:T(8,128)(2,1)} %get-tuple-element.17) | copy-start | bytes 983044
  181.2 2.8 %copy-start.9 = (bf16[1,64,2560]{2,1,0:T(8,128)(2,1)S(1)}, bf16[1,64,2560]{2,1,0:T(8,128)(2,1)}, u32[]{:S(2)}) copy-start(bf16[1,64,2560]{2,1,0:T(8,128)(2,1)} %get-tuple-element.18) | copy-start | bytes 983044
  181.2 3.5 %copy-start.8 = (bf16[1,64,2560]{2,1,0:T(8,128)(2,1)S(1)}, bf16[1,64,2560]{2,1,0:T(8,128)(2,1)}, u32[]{:S(2)}) copy-start(bf16[1,64,2560]{2,1,0:T(8,128)(2,1)} %get-tuple-element.19) | copy-start | bytes 983044

commit v4 on v3

--- a/solution.py
+++ b/solution.py
@@ -52,23 +52,35 @@
 ARRIVALS = (
     (0, 0, 0),
     (0, 0, 1),
-    (1, 0, 0),
     (0, 3, 0),
     (0, 1, 0),
-    (1, 1, 0),
-    (1, 3, 0),
+    (1, 0, 0),
     (0, 2, 0),
-    (1, 2, 0),
-    (1, 0, 1),
     (0, 3, 1),
     (0, 1, 1),
+    (1, 0, 1),
+    (0, 2, 1),
+    (1, 3, 0),
+    (1, 1, 0),
+    (1, 2, 0),
+    (1, 3, 1),
     (1, 1, 1),
-    (1, 3, 1),
-    (0, 2, 1),
     (1, 2, 1),
 )
-WEIGHTS_START = 1
-WEIGHTS_PASS = 13
+PASS_TURNS = {
+    (0, 3, 0): 2,
+    (0, 1, 0): 2,
+    (1, 0, 0): 4,
+    (0, 2, 0): 4,
+    (1, 3, 0): 10,
+    (1, 1, 0): 11,
+    (1, 2, 0): 12,
+}
+ODD_LAG = 2
+WEIGHTS_START = 2
+PUSH_START = 5
+WEIGHTS_PASS = 11
+WEIGHTS_LAST = 15
 
 
 def attention_kernel(
@@ -77,11 +89,11 @@
     grads_ref,
     gate_ref,
     up_ref,
-    down_ref,
     heads_out,
     grads_out,
     weights_out,
     kv_all,
+    odd_out,
     odd_in,
     turned,
     m_ref,
@@ -99,8 +111,8 @@
     local_sem,
 ):
     zl, y, c, ex = (lax.axis_index(a) for a in (*SEQ, "exp"))
-    half_rows = odd_in.shape[0]
-    heads = odd_in.shape[1] // HEAD_DIM
+    half_rows = odd_in.shape[1]
+    heads = odd_in.shape[0] // HEAD_DIM
     pieces = half_rows // 128
     experts = grads_ref.shape[0]
     shard = zl * 8 + y * 2 + c
@@ -109,12 +121,13 @@
     z_peer = neighbour(zl=1 - zl)
     y_up = neighbour(y=lax.rem(y + 1, 4))
     y_down = neighbour(y=lax.rem(y + 3, 4))
+    y_far = neighbour(y=lax.rem(y + 2, 4))
 
     def mirrored(e):
         return {"zl": 1 - zl, "y": 3 - y, "c": 1 - c, "exp": e}
 
     barrier = pltpu.get_barrier_semaphore()
-    greeted = [core_peer, y_up, y_down]
+    greeted = [core_peer, y_up, y_down, y_far]
     for d in range(experts):
         e = lax.rem(ex + d, experts)
         greeted += [mirrored(e), neighbour(zl=1 - zl, exp=e)]
@@ -125,7 +138,7 @@
 
     own_weights = [
         pltpu.make_async_copy(ref.at[0], weights_out.at[n, c, y], local_sem.at[n])
-        for n, ref in enumerate((gate_ref, up_ref, down_ref))
+        for n, ref in enumerate((gate_ref, up_ref))
     ]
     own_grads = pltpu.make_async_copy(grads_ref.at[ex], grads_out.at[zl, ex], local_sem.at[3])
     for copy in (*own_weights, own_grads):
@@ -141,8 +154,7 @@
             :, p * 128 : (p + 1) * 128
         ]
 
-    def turn(half, rows):
-        flipped = rows.T
+    def turn(half, flipped):
         flat = jnp.concatenate(
             [flipped[h * HEAD_DIM : (h + 1) * HEAD_DIM] for h in range(heads)], axis=1
         )
@@ -150,13 +162,14 @@
         turned[half, 0] = jnp.concatenate([flat, empty], axis=0)
         turned[half, 1] = jnp.concatenate([empty, flat], axis=0)
 
-    turn(0, queries_ref[pl.ds(0, half_rows), :])
+    odd_out[...] = queries_ref[pl.ds(half_rows, half_rows), :].T
+    turn(0, queries_ref[pl.ds(0, half_rows), :].T)
     m_ref[...] = jnp.full_like(m_ref, very_negative)
     acc_ref[...] = jnp.zeros_like(acc_ref)
     pl.semaphore_wait(barrier, len(greeted))
 
     odd_copy = pltpu.make_async_remote_copy(
-        src_ref=queries_ref.at[pl.ds(half_rows, half_rows)],
+        src_ref=odd_out,
         dst_ref=odd_in,
         send_sem=odd_sem.at[0],
         recv_sem=odd_sem.at[1],
@@ -178,13 +191,13 @@
         )
 
     routes = {
-        (0, 0, 0): (z_peer, y_up, y_down, core_peer),
-        (1, 0, 0): (y_up, y_down, core_peer),
-        (0, 3, 0): (y_up, core_peer),
-        (0, 1, 0): (core_peer,),
-        (1, 1, 0): (y_down, core_peer),
+        (0, 0, 0): (z_peer, y_up, y_down, y_far, core_peer),
+        (0, 3, 0): (z_peer, core_peer),
+        (0, 1, 0): (z_peer, core_peer),
+        (0, 2, 0): (z_peer, core_peer),
+        (1, 0, 0): (core_peer,),
         (1, 3, 0): (core_peer,),
-        (0, 2, 0): (core_peer,),
+        (1, 1, 0): (core_peer,),
         (1, 2, 0): (core_peer,),
     }
     forwards = {}
@@ -235,9 +248,9 @@
             )
         )
 
+    odd_copy.start()
     for copy in forwards[(0, 0, 0)]:
         copy.start()
-    odd_copy.start()
 
     ones = jnp.ones((16, half_rows), jnp.bfloat16)
 
@@ -273,34 +286,46 @@
         acc_ref[half] = total
 
     step(0, shard, 1, True)
-    odd_copy.wait_recv()
-    turn(1, odd_in[...])
-
-    def visit(slot, carry):
+
+    def slot_shard(slot):
         def pick(axis):
             return sum(
                 jnp.where(slot == n, place[axis], 0) for n, place in enumerate(ARRIVALS)
             )
 
-        t = shard_at(pick(0), pick(1), pick(2))
-
-        @pl.when(slot > 0)
-        def _():
-            pass_on(0, t, core_peer).wait_recv()
-
+        return shard_at(pick(0), pick(1), pick(2))
+
+    def visit(slot, carry):
         for n, place in enumerate(ARRIVALS):
-            if n and place in forwards:
+            if place in PASS_TURNS:
+
+                @pl.when(slot == PASS_TURNS[place])
+                def _():
+                    pass_on(0, shard_at(*place), core_peer).wait_recv()
+                    for copy in forwards[place]:
+                        copy.start()
+
+            elif n:
 
                 @pl.when(slot == n)
                 def _():
-                    for copy in forwards[place]:
-                        copy.start()
+                    pass_on(0, shard_at(*place), core_peer).wait_recv()
+
+        @pl.when(slot == ODD_LAG)
+        def _():
+            odd_copy.wait_recv()
+            turn(1, odd_in[...])
 
         @pl.when(slot == WEIGHTS_START)
         def _():
             for copy in own_weights:
                 copy.wait()
-            for copy in (*weight_own, *pushes):
+            for copy in weight_own:
+                copy.start()
+
+        @pl.when(slot == PUSH_START)
+        def _():
+            for copy in pushes:
                 copy.start()
 
         @pl.when(slot == WEIGHTS_PASS)
@@ -312,8 +337,18 @@
             weight_below.start()
             weight_core[1].start()
 
+        @pl.when(slot == WEIGHTS_LAST)
+        def _():
+            weight_above.wait_recv()
+            weight_below.wait_recv()
+            weight_core[2].start()
+
         def one_half(half, inner):
-            @pl.when(t < jnp.where(half == 0, shard, mirror))
+            seen = slot - ODD_LAG * half
+            t = slot_shard(seen)
+            here = (seen >= 0) & (seen < len(ARRIVALS))
+
+            @pl.when(here & (t < jnp.where(half == 0, shard, mirror)))
             def _():
                 step(half, t, 2, False)
 
@@ -322,20 +357,22 @@
         lax.fori_loop(0, 2, one_half, 0)
         return carry
 
-    lax.fori_loop(0, len(ARRIVALS), visit, 0)
+    lax.fori_loop(0, len(ARRIVALS) + ODD_LAG, visit, 0)
     step(1, mirror, 2, True)
 
     for half in range(2):
         total = acc_ref[half]
         mixed = total[:HEAD_DIM] / total[HEAD_DIM : HEAD_DIM + 1]
         for head in range(heads):
-            mixed_ref[half, :, pl.ds(head * HEAD_DIM, HEAD_DIM)] = (
-                mixed[:, head * half_rows : (head + 1) * half_rows].T.astype(jnp.bfloat16)
-            )
+            for block in range(pieces):
+                start = head * half_rows + block * 128
+                mixed_ref[half, block, pl.ds(head * HEAD_DIM, HEAD_DIM), :] = mixed[
+                    :, start : start + 128
+                ].astype(jnp.bfloat16)
 
     def head_copy(half, block, to):
         return pltpu.make_async_remote_copy(
-            src_ref=mixed_ref.at[half, pl.ds(pl.multiple_of(block * 128, 128), 128)],
+            src_ref=mixed_ref.at[half, block],
             dst_ref=heads_out.at[ex],
             send_sem=heads_send.at[half, block],
             recv_sem=heads_recv.at[ex],
@@ -352,9 +389,7 @@
         block = lax.rem(ex + d, 4)
         odd_copies.append(head_copy(1, block, mirrored(4 + block)))
     own_heads = pltpu.make_async_copy(
-        mixed_ref.at[0, pl.ds(pl.multiple_of(lax.rem(ex, 4) * 128, 128), 128)],
-        heads_out.at[ex],
-        local_sem.at[4],
+        mixed_ref.at[0, lax.rem(ex, 4)], heads_out.at[ex], local_sem.at[4]
     )
     for copy in (*odd_copies, *even_copies[1:]):
         copy.start()
@@ -367,13 +402,9 @@
     def _():
         even_copies[0].start()
 
-    weight_above.wait_recv()
-    weight_below.wait_recv()
-    weight_core[2].start()
-
     def head_arrival(e):
         return pltpu.make_async_remote_copy(
-            src_ref=mixed_ref.at[0, pl.ds(0, 128)],
+            src_ref=mixed_ref.at[0, 0],
             dst_ref=heads_out.at[e],
             send_sem=heads_send.at[0, 0],
             recv_sem=heads_recv.at[e],
@@ -409,7 +440,7 @@
         copy.wait_send()
 
 
-def attend(queries, keyvals, send_grads, w_gate, w_up, w_down):
+def attend(queries, keyvals, send_grads, w_gate, w_up):
     row_count, query_width = queries.shape
     half_rows = row_count // 2
     heads = query_width // HEAD_DIM
@@ -422,19 +453,20 @@
     return pl.pallas_call(
         attention_kernel,
         out_shape=(
-            jax.ShapeDtypeStruct((experts, row_count // experts, query_width), bf16),
+            jax.ShapeDtypeStruct((experts, query_width, row_count // experts), bf16),
             jax.ShapeDtypeStruct((2, experts, capacity, width), bf16),
-            jax.ShapeDtypeStruct((3, 2, 4, owned, width), bf16),
+            jax.ShapeDtypeStruct((2, 2, 4, owned, width), bf16),
         ),
-        in_specs=[vmem] * 2 + [anywhere] * 4,
+        in_specs=[vmem] * 2 + [anywhere] * 3,
         out_specs=(anywhere,) * 3,
         scratch_shapes=[
             pltpu.VMEM((len(ARRIVALS), row_count, 2 * HEAD_DIM), bf16),
-            pltpu.VMEM((half_rows, query_width), bf16),
+            pltpu.VMEM((query_width, half_rows), bf16),
+            pltpu.VMEM((query_width, half_rows), bf16),
             pltpu.VMEM((2, 2, 2 * HEAD_DIM, heads * half_rows), bf16),
             pltpu.VMEM((2, 1, heads * half_rows), jnp.float32),
             pltpu.VMEM((2, HEAD_DIM + 16, heads * half_rows), jnp.float32),
-            pltpu.VMEM((2, half_rows, query_width), bf16),
+            pltpu.VMEM((2, half_rows // 128, query_width, 128), bf16),
             dma((15,)),
             dma((len(ARRIVALS),)),
             dma((2,)),
@@ -453,13 +485,14 @@
             flops=20_000_000_000, bytes_accessed=20_000_000, transcendentals=27_000_000
         ),
         name="attention",
-    )(queries, keyvals, send_grads, w_gate, w_up, w_down)
+    )(queries, keyvals, send_grads, w_gate, w_up)
 
 
 def expert_kernel(
     rows_ref,
     cot_in,
     weights_ref,
+    own_down_ref,
     hidden_ref,
     combine_ref,
     layer_ref,
@@ -467,6 +500,7 @@
     grad_up_ref,
     grad_down_ref,
     rows_in,
+    down_in,
     out_buf,
     out_in,
     parts,
@@ -480,6 +514,8 @@
     push_recv,
     ring_send,
     ring_recv,
+    weight_send,
+    weight_recv,
     local_sem,
 ):
     zl, y, c, ex = (lax.axis_index(a) for a in (*SEQ, "exp"))
@@ -497,6 +533,7 @@
     def source(dz, de):
         return lax.rem(zl + 2 - dz, 2), lax.rem(ex + experts - de, experts)
 
+    down_in[c, y] = own_down_ref[0]
     barrier = pltpu.get_barrier_semaphore()
     for dz, de in offsets[1:]:
         tz, te = peer(dz, de)
@@ -609,7 +646,37 @@
             jnp.bfloat16
         )
 
-    gate, up, down = (weights_ref[n].reshape(-1, width) for n in range(3))
+    def weight_copy(index, rows, dy, to):
+        part = down_in.at[c, lax.rem(y + dy, 4), rows]
+        return pltpu.make_async_remote_copy(
+            src_ref=part,
+            dst_ref=part,
+            send_sem=weight_send.at[index],
+            recv_sem=weight_recv.at[index],
+            device_id=to,
+            device_id_type=MESH,
+        )
+
+    owned = down_in.shape[2]
+    every, low, high = pl.ds(0, owned), pl.ds(0, owned // 2), pl.ds(owned // 2, owned // 2)
+    weight_own = [
+        go(weight_copy(0, every, 0, y_up)),
+        go(weight_copy(1, every, 0, y_down)),
+        go(weight_copy(2, every, 0, core_peer)),
+    ]
+    weight_own[0].wait_recv()
+    weight_above = go(weight_copy(3, low, 3, y_up))
+    weight_core = [go(weight_copy(5, every, 3, core_peer))]
+    weight_own[1].wait_recv()
+    weight_below = go(weight_copy(4, high, 1, y_down))
+    weight_core.append(go(weight_copy(6, every, 1, core_peer)))
+    weight_above.wait_recv()
+    weight_below.wait_recv()
+    weight_core.append(go(weight_copy(7, every, 2, core_peer)))
+    for copy in (weight_own[2], *weight_core):
+        copy.wait_recv()
+    gate, up = (weights_ref[n].reshape(-1, width) for n in range(2))
+    down = down_in[...].reshape(-1, width)
     output_grads = flat(cot_in)
     hidden_grad = contract_cols(output_grads, down)
     arrive(rows_copies)
@@ -666,7 +733,7 @@
         copy.wait_send()
 
 
-def expert_layer(send_rows, grad_rows, weights, hidden_state, dispatch_table):
+def expert_layer(send_rows, grad_rows, weights, w_down, hidden_state, dispatch_table):
     experts, capacity, width = send_rows.shape
     owned = weights.shape[3]
     token_count = hidden_state.shape[0]
@@ -678,10 +745,11 @@
     return pl.pallas_call(
         expert_kernel,
         out_shape=(jax.ShapeDtypeStruct((token_count, width), bf16),) + (grad_shape,) * 3,
-        in_specs=[vmem] * 5,
+        in_specs=[vmem] * 6,
         out_specs=(vmem,) * 4,
         scratch_shapes=[
             landing,
+            pltpu.VMEM((2, 4, owned, width), bf16),
             landing,
             landing,
             pltpu.VMEM((3, 2, 4, owned, width), bf16),
@@ -695,6 +763,8 @@
             pltpu.SemaphoreType.DMA((3, 2 * experts)),
             pltpu.SemaphoreType.DMA((3, 5)),
             pltpu.SemaphoreType.DMA((3, 5)),
+            pltpu.SemaphoreType.DMA((8,)),
+            pltpu.SemaphoreType.DMA((8,)),
             pltpu.SemaphoreType.DMA((3,)),
         ],
         compiler_params=pltpu.CompilerParams(
@@ -704,7 +774,7 @@
             flops=5_000_000_000, bytes_accessed=20_000_000, transcendentals=200_000
         ),
         name="experts",
-    )(send_rows, grad_rows, weights, hidden_state, combine)
+    )(send_rows, grad_rows, weights, w_down, hidden_state, combine)
 
 
 def local(
@@ -743,20 +813,18 @@
         )
 
     token_heads, grad_rows, weights = attend(
-        queries, keyvals, placed(cotangent), w_gate, w_up, w_down
-    )
-    projected = jnp.dot(
-        jnp.transpose(token_heads, (1, 0, 2)).reshape(token_count, -1),
-        out_proj,
-        preferred_element_type=jnp.float32,
-    )
+        queries, keyvals, placed(cotangent), w_gate, w_up
+    )
+    projected = contract_rows(token_heads.reshape(-1, token_count), out_proj)
     hidden_state = (resid.astype(jnp.float32) + projected).astype(jnp.bfloat16)
     widened = hidden_state.astype(jnp.float32)
     mean_square = jnp.mean(widened * widened, axis=1, keepdims=True)
     normed = (widened * lax.rsqrt(mean_square + norm_eps) * norm_gain.astype(jnp.float32)).astype(
         jnp.bfloat16
     )
-    return expert_layer(placed(normed), grad_rows, weights, hidden_state, dispatch_table)
+    return expert_layer(
+        placed(normed), grad_rows, weights, w_down, hidden_state, dispatch_table
+    )
 
 
 def solution(mesh):

time: 186 us -> 168 us (0.903)
  Pallas kernels: 165 us -> 153 us
  matrix products: 6.28 us -> 3.06 us
  local copies, waits for them, and re-layouts: 9.66 us -> 7.44 us
    pallas_call x1, Pallas kernels: 97 us -> 83.1 us  [attend(): pl.pallas_call(attention_kernel, out_shape=(jax.ShapeDtypeStruct((experts...]
    dot_general x1, matrix products: 4.55 us -> 1.32 us  [contract_rows(): lax.dot_general(first_operand, second_operand, (((0,), (0,)), ((), ())),...]
    pallas_call x1, Pallas kernels: 68.3 us -> 70.4 us  [expert_layer(): pl.pallas_call(expert_kernel, out_shape=(jax.ShapeDtypeStruct((token_coun...]
    unnamed x27 -> x29, local copies, waits for them, and re-layouts: 7.44 us -> 5.48 us
where the time goes in v4:
time: 168 us
  Pallas kernels  153 us (91%)
  local copies, waits for them, and re-layouts  7.44 us (4%)
  other arithmetic  3.33 us (2%)
  matrix products  3.06 us (2%)
    pallas_call x1, Pallas kernels, attend(): pl.pallas_call(attention_kernel, out_shape=(jax.ShapeDtypeStruct((experts...  83.1 us
    pallas_call x1, Pallas kernels, expert_layer(): pl.pallas_call(expert_kernel, out_shape=(jax.ShapeDtypeStruct((token_coun...  70.4 us
    unnamed x29, local copies, waits for them, and re-layouts  5.48 us

profile of v4, /device:TPU:1, one launch (start us, length us, event | category | flops | bytes accessed | tf_op | source)
XLA Modules:
  0.0 168.1 jit_solution(13315397354609114922)
XLA Ops:
  0.6 0.0 copy-start
  0.6 0.7 compare_select_fusion
  1.4 2.0 %gather_fusion = s32[128]{0:T(128)S(1)} fusion(s32[128256]{0:T(1024)} %param.17, s32[1024]{0:T(1024)S(1)} %pad_clamp_fusion), kind=kCustom, calls=%fused_computation | custom fusion | bytes 1536 | tf_op jit(solution)/shard_map/jit(_take)/gather | solution.py:797
  3.3 0.0 copy-start.1
  3.3 0.0 copy-start.2
  3.4 0.0 copy-start.3
  3.4 0.7 and_select_fusion
  4.1 0.7 convert_element_type.30
  4.8 0.1 fusion.8
  4.9 0.2 reduce_window_sum.11
  5.1 0.2 select_reduce_fusion
  5.3 0.1 iota_compare_fusion.1
  5.3 0.6 fusion.7.combine_ref
  6.0 1.2 copy.16.queries_ref
  7.2 0.0 copy-done
  7.2 0.4 convolution_convert_fusion.1
  7.7 0.0 slice-start
  7.7 0.0 copy-done.1
  7.7 0.0 copy-done.2
  7.7 0.0 copy-done.3
  7.7 0.0 slice-start.1
  7.7 0.0 copy-start.6
  7.7 83.1 %attention.1 = (bf16[8,192,128]{2,1,0:T(8,128)(2,1)S(1)}, bf16[2,8,16,2560]{3,2,1,0:T(8,128)(2,1)S(1)}, bf16[2,2,4,64,2560]{4,3,2,1,0:T(8,128)(2,1)}) custom-call(bf16[1024,192]{1,0:T(8,128)(2,1)S(1)} %copy.16.queries_ref, bf16[1024,128]{1,0:T(8,128)(2,1)S(1)} %copy-done.3, bf16[8,16,2560]{2,1,0:T(8,128)(2,1)S(1)} %bitcast.9, ...), custom_call_target="tpu_custom_call" | custom-call | flops 20000000000 | bytes 20000000 | tf_op jit(solution)/shard_map/attention/pallas_call | solution.py:453
  90.8 0.0 copy-start.4
  90.8 0.0 slice-done
  90.8 0.0 slice-done.1
  90.8 0.0 copy-done.6
  90.9 1.3 fusion.1
  92.2 0.0 copy-done.4
  92.2 0.0 copy-start.5
  92.2 1.3 convolution_convert_fusion
  93.5 0.0 copy-done.5
  93.5 70.4 %experts.1 = (bf16[128,2560]{1,0:T(8,128)(2,1)}, bf16[1,64,2560]{2,1,0:T(8,128)(2,1)}, bf16[1,64,2560]{2,1,0:T(8,128)(2,1)}, bf16[1,64,2560]{2,1,0:T(8,128)(2,1)}) custom-call(bf16[8,16,2560]{2,1,0:T(8,128)(2,1)} %bitcast.12, bf16[2,8,16,2560]{3,2,1,0:T(8,128)(2,1)} %copy-done.4, bf16[2,2,4,64,2560]{4,3,2,1,0:T(8,128)(2,1)} %get-tuple-element.9.weights_ref, ...), custom_call_target="tpu_custom_call" | custom-call | flops 5000000000 | bytes 20000000 | tf_op jit(solution)/shard_map/experts/pallas_call | solution.py:745
  163.9 0.0 copy-start.9
  163.9 0.0 copy-start.8
  163.9 0.0 copy-start.7
  163.9 2.0 %copy.21 = bf16[128,2560]{1,0:T(8,128)(2,1)} copy(bf16[128,2560]{1,0:T(8,128)(2,1)} %get-tuple-element.16) | data formatting | bytes 1310720
  166.0 0.0 copy-done.9
  166.0 0.7 copy.22
  166.7 0.0 copy-done.8
  166.7 0.7 copy.23
  167.4 0.0 copy-done.7
  167.4 0.7 copy.24
  (4 shorter events, 0.0 us)
Async XLA Ops:
  0.6 6.6 %copy-start = (bf16[128,2560]{1,0:T(8,128)(2,1)S(1)}, bf16[128,2560]{1,0:T(8,128)(2,1)}, u32[]{:S(2)}) copy-start(bf16[128,2560]{1,0:T(8,128)(2,1)} %param.21) | copy-start | bytes 1966084
  3.3 4.3 %copy-start.1 = (bf16[1,64,2560]{2,1,0:T(8,128)(2,1)S(1)}, bf16[1,64,2560]{2,1,0:T(8,128)(2,1)}, u32[]{:S(2)}) copy-start(bf16[1,64,2560]{2,1,0:T(8,128)(2,1)} %gate_ref.1) | copy-start | bytes 983044
  3.3 4.3 %copy-start.2 = (bf16[1,64,2560]{2,1,0:T(8,128)(2,1)S(1)}, bf16[1,64,2560]{2,1,0:T(8,128)(2,1)}, u32[]{:S(2)}) copy-start(bf16[1,64,2560]{2,1,0:T(8,128)(2,1)} %up_ref.1) | copy-start | bytes 983044
  3.4 4.3 %copy-start.3 = (bf16[1024,128]{1,0:T(8,128)(2,1)S(1)}, bf16[1024,128]{1,0:T(8,128)(2,1)}, u32[]{:S(2)}) copy-start(bf16[1024,128]{1,0:T(8,128)(2,1)} %keyvals_ref.1) | copy-start | bytes 786436
  7.7 83.2 %slice-start = ((s8[7864320]{0:T(1024)(128)(4,1)}), s8[4194304]{0:T(1024)(128)(4,1)S(1)}, s32[]{:S(2)}) async-start(s8[7864320]{0:T(1024)(128)(4,1)} %bitcast.10), calls=%async_computation | async-start | bytes 8388608
  7.7 83.1 %slice-start.1 = ((s8[7864320]{0:T(1024)(128)(4,1)}), s8[3670016]{0:T(1024)(128)(4,1)S(1)}, s32[]{:S(2)}) async-start(s8[7864320]{0:T(1024)(128)(4,1)} %bitcast.10), calls=%async_computation.1 | async-start | bytes 7340032
  7.7 83.1 %copy-start.6 = (bf16[128,2560]{1,0:T(8,128)(2,1)S(1)}, bf16[128,2560]{1,0:T(8,128)(2,1)}, u32[]{:S(2)}) copy-start(bf16[128,2560]{1,0:T(8,128)(2,1)} %param.11) | copy-start | bytes 1966084
  90.8 1.4 copy-start.4
  92.2 1.3 copy-start.5
  163.9 2.1 %copy-start.9 = (bf16[1,64,2560]{2,1,0:T(8,128)(2,1)S(1)}, bf16[1,64,2560]{2,1,0:T(8,128)(2,1)}, u32[]{:S(2)}) copy-start(bf16[1,64,2560]{2,1,0:T(8,128)(2,1)} %get-tuple-element.17) | copy-start | bytes 983044
  163.9 2.8 %copy-start.8 = (bf16[1,64,2560]{2,1,0:T(8,128)(2,1)S(1)}, bf16[1,64,2560]{2,1,0:T(8,128)(2,1)}, u32[]{:S(2)}) copy-start(bf16[1,64,2560]{2,1,0:T(8,128)(2,1)} %get-tuple-element.18) | copy-start | bytes 983044
  163.9 3.5 %copy-start.7 = (bf16[1,64,2560]{2,1,0:T(8,128)(2,1)S(1)}, bf16[1,64,2560]{2,1,0:T(8,128)(2,1)}, u32[]{:S(2)}) copy-start(bf16[1,64,2560]{2,1,0:T(8,128)(2,1)} %get-tuple-element.19) | copy-start | bytes 983044

commit v5 on v4

--- a/solution.py
+++ b/solution.py
@@ -59,10 +59,10 @@
     (0, 3, 1),
     (0, 1, 1),
     (1, 0, 1),
-    (0, 2, 1),
     (1, 3, 0),
     (1, 1, 0),
     (1, 2, 0),
+    (0, 2, 1),
     (1, 3, 1),
     (1, 1, 1),
     (1, 2, 1),
@@ -71,16 +71,18 @@
     (0, 3, 0): 2,
     (0, 1, 0): 2,
     (1, 0, 0): 4,
-    (0, 2, 0): 4,
-    (1, 3, 0): 10,
-    (1, 1, 0): 11,
-    (1, 2, 0): 12,
+    (0, 2, 0): 5,
+    (1, 3, 0): 7,
+    (1, 1, 0): 8,
+    (1, 2, 0): 8,
 }
+KEY_PIECE = 256
 ODD_LAG = 2
-WEIGHTS_START = 2
-PUSH_START = 5
-WEIGHTS_PASS = 11
-WEIGHTS_LAST = 15
+FAR_START = 2
+WEIGHTS_START = 4
+PUSH_START = 9
+WEIGHTS_PASS = 14
+WEIGHTS_LAST = 17
 
 
 def attention_kernel(
@@ -97,6 +99,8 @@
     odd_in,
     turned,
     m_ref,
+    peak_ref,
+    scores_ref,
     acc_ref,
     mixed_ref,
     kv_send,
@@ -191,11 +195,11 @@
         )
 
     routes = {
-        (0, 0, 0): (z_peer, y_up, y_down, y_far, core_peer),
+        (0, 0, 0): (z_peer, y_up, y_down, core_peer, y_far),
         (0, 3, 0): (z_peer, core_peer),
         (0, 1, 0): (z_peer, core_peer),
-        (0, 2, 0): (z_peer, core_peer),
-        (1, 0, 0): (core_peer,),
+        (1, 0, 0): (y_far, core_peer),
+        (0, 2, 0): (core_peer,),
         (1, 3, 0): (core_peer,),
         (1, 1, 0): (core_peer,),
         (1, 2, 0): (core_peer,),
@@ -249,7 +253,7 @@
         )
 
     odd_copy.start()
-    for copy in forwards[(0, 0, 0)]:
+    for copy in forwards[(0, 0, 0)][:4]:
         copy.start()
 
     ones = jnp.ones((16, half_rows), jnp.bfloat16)
@@ -261,31 +265,64 @@
         ]
         return jnp.concatenate([jnp.concatenate(turned_values, axis=1), ones], axis=0)
 
-    def step(half, block, parts, masked):
-        keys = kv_all[block, pl.ds(0, half_rows), :]
-        scores = []
-        for part in range(parts):
-            s = (
-                jnp.dot(keys, turned[half, part], preferred_element_type=jnp.float32)
-                * score_to_log2
+    def columns(head):
+        return slice(head * half_rows, (head + 1) * half_rows)
+
+    key_pieces = [pl.ds(start, KEY_PIECE) for start in range(0, half_rows, KEY_PIECE)]
+
+    def score(half, block, part, rows, head, masked):
+        s = (
+            jnp.dot(
+                kv_all[block, rows, :],
+                turned[half, part, :, columns(head)],
+                preferred_element_type=jnp.float32,
             )
-            if masked and part == parts - 1:
-                key_place = lax.broadcasted_iota(jnp.int32, s.shape, 0)
-                query_place = lax.broadcasted_iota(jnp.int32, s.shape, 1) % half_rows
-                s = jnp.where(key_place <= query_place, s, very_negative)
-            scores.append(s)
-        old = m_ref[half]
-        new = old
-        for s in scores:
-            new = jnp.maximum(new, jnp.max(s, axis=0, keepdims=True))
+            * score_to_log2
+        )
+        if masked:
+            key_place = rows.start + lax.broadcasted_iota(jnp.int32, s.shape, 0)
+            query_place = lax.broadcasted_iota(jnp.int32, s.shape, 1)
+            s = jnp.where(key_place <= query_place, s, very_negative)
+        return s
+
+    def stage(slot, half, block, following=None):
+        new = peak_ref[...]
+        shrink = jnp.exp2(m_ref[half] - new)
         m_ref[half] = new
-        total = acc_ref[half] * jnp.exp2(old - new)
-        for part, s in enumerate(scores):
-            weights = jnp.exp2(s - new).astype(jnp.bfloat16)
-            total += jnp.dot(values_of(block, part), weights, preferred_element_type=jnp.float32)
-        acc_ref[half] = total
-
-    step(0, shard, 1, True)
+        if following is not None:
+            next_half, next_block, masked = following
+            start = m_ref[next_half]
+        for head in range(heads):
+            cols = columns(head)
+            total = acc_ref[half, :, cols] * shrink[:, cols]
+            if following is not None:
+                peak = start[:, cols]
+            for part in range(2):
+                values = values_of(block, part)
+                for rows in key_pieces:
+                    if following is not None:
+                        s = score(next_half, next_block, part, rows, head, masked and part == 1)
+                        scores_ref[1 - slot, part, rows, cols] = s
+                        peak = jnp.maximum(peak, jnp.max(s, axis=0, keepdims=True))
+                    weights = jnp.exp2(scores_ref[slot, part, rows, cols] - new[:, cols])
+                    total += jnp.dot(
+                        values[:, rows.start : rows.start + KEY_PIECE],
+                        weights.astype(jnp.bfloat16),
+                        preferred_element_type=jnp.float32,
+                    )
+            acc_ref[half, :, cols] = total
+            if following is not None:
+                peak_ref[:, cols] = peak
+
+    for head in range(heads):
+        cols = columns(head)
+        peak = m_ref[0, :, cols]
+        for rows in key_pieces:
+            s = score(0, shard, 0, rows, head, True)
+            scores_ref[0, 0, rows, cols] = s
+            scores_ref[0, 1, rows, cols] = jnp.full_like(s, very_negative)
+            peak = jnp.maximum(peak, jnp.max(s, axis=0, keepdims=True))
+        peak_ref[:, cols] = peak
 
     def slot_shard(slot):
         def pick(axis):
@@ -310,6 +347,10 @@
                 @pl.when(slot == n)
                 def _():
                     pass_on(0, shard_at(*place), core_peer).wait_recv()
+
+        @pl.when(slot == FAR_START)
+        def _():
+            forwards[(0, 0, 0)][4].start()
 
         @pl.when(slot == ODD_LAG)
         def _():
@@ -344,21 +385,31 @@
             weight_core[2].start()
 
         def one_half(half, inner):
+            last_half, last_block, scored = inner
             seen = slot - ODD_LAG * half
             t = slot_shard(seen)
             here = (seen >= 0) & (seen < len(ARRIVALS))
 
-            @pl.when(here & (t < jnp.where(half == 0, shard, mirror)))
-            def _():
-                step(half, t, 2, False)
-
-            return inner
-
-        lax.fori_loop(0, 2, one_half, 0)
-        return carry
-
-    lax.fori_loop(0, len(ARRIVALS) + ODD_LAG, visit, 0)
-    step(1, mirror, 2, True)
+            used = here & (t < jnp.where(half == 0, shard, mirror))
+            for now in range(2):
+
+                @pl.when(used & (scored == now))
+                def _():
+                    stage(now, last_half, last_block, (half, t, False))
+
+            return (
+                jnp.where(used, half, last_half),
+                jnp.where(used, t, last_block),
+                jnp.where(used, 1 - scored, scored),
+            )
+
+        return lax.fori_loop(0, 2, one_half, carry)
+
+    last_half, last_block, _ = lax.fori_loop(
+        0, len(ARRIVALS) + ODD_LAG, visit, (jnp.int32(0), shard, jnp.int32(0))
+    )
+    stage(1, last_half, last_block, (1, mirror, True))
+    stage(0, 1, mirror)
 
     for half in range(2):
         total = acc_ref[half]
@@ -465,6 +516,8 @@
             pltpu.VMEM((query_width, half_rows), bf16),
             pltpu.VMEM((2, 2, 2 * HEAD_DIM, heads * half_rows), bf16),
             pltpu.VMEM((2, 1, heads * half_rows), jnp.float32),
+            pltpu.VMEM((1, heads * half_rows), jnp.float32),
+            pltpu.VMEM((2, 2, half_rows, heads * half_rows), jnp.float32),
             pltpu.VMEM((2, HEAD_DIM + 16, heads * half_rows), jnp.float32),
             pltpu.VMEM((2, half_rows // 128, query_width, 128), bf16),
             dma((15,)),

time: 168 us -> 154 us (0.917)
  Pallas kernels: 153 us -> 139 us
    pallas_call x1, Pallas kernels: 83.1 us -> 74.3 us  [attend(): pl.pallas_call(attention_kernel, out_shape=(jax.ShapeDtypeStruct((experts...]
    pallas_call x1, Pallas kernels: 70.4 us -> 64.4 us  [expert_layer(): pl.pallas_call(expert_kernel, out_shape=(jax.ShapeDtypeStruct((token_coun...]
where the time goes in v5:
time: 154 us; the launch traced here: 153 us
  Pallas kernels  139 us (90%)
  local copies, waits for them, and re-layouts  7.44 us (5%)
  other arithmetic  3.33 us (2%)
  matrix products  3.06 us (2%)
    pallas_call x1, Pallas kernels, attend(): pl.pallas_call(attention_kernel, out_shape=(jax.ShapeDtypeStruct((experts...  74.3 us
    pallas_call x1, Pallas kernels, expert_layer(): pl.pallas_call(expert_kernel, out_shape=(jax.ShapeDtypeStruct((token_coun...  64.4 us
    unnamed x29, local copies, waits for them, and re-layouts  5.48 us

profile of v5, /device:TPU:1, one launch (start us, length us, event | category | flops | bytes accessed | tf_op | source)
XLA Modules:
  0.0 153.3 jit_solution(3150627179296423663)
XLA Ops:
  0.6 0.0 copy-start
  0.6 0.7 compare_select_fusion
  1.4 2.0 %gather_fusion = s32[128]{0:T(128)S(1)} fusion(s32[128256]{0:T(1024)} %param.17, s32[1024]{0:T(1024)S(1)} %pad_clamp_fusion), kind=kCustom, calls=%fused_computation | custom fusion | bytes 1536 | tf_op jit(solution)/shard_map/jit(_take)/gather | solution.py:850
  3.3 0.0 copy-start.1
  3.3 0.0 copy-start.2
  3.4 0.0 copy-start.3
  3.4 0.7 and_select_fusion
  4.1 0.7 convert_element_type.30
  4.8 0.1 fusion.8
  4.9 0.2 reduce_window_sum.11
  5.1 0.2 select_reduce_fusion
  5.3 0.1 iota_compare_fusion.1
  5.3 0.6 fusion.7.combine_ref
  6.0 1.2 copy.16.queries_ref
  7.2 0.0 copy-done
  7.2 0.4 convolution_convert_fusion.1
  7.7 0.0 slice-start
  7.7 0.0 copy-done.1
  7.7 0.0 copy-done.2
  7.7 0.0 copy-done.3
  7.7 0.0 slice-start.1
  7.7 0.0 copy-start.6
  7.7 74.3 %attention.1 = (bf16[8,192,128]{2,1,0:T(8,128)(2,1)S(1)}, bf16[2,8,16,2560]{3,2,1,0:T(8,128)(2,1)S(1)}, bf16[2,2,4,64,2560]{4,3,2,1,0:T(8,128)(2,1)}) custom-call(bf16[1024,192]{1,0:T(8,128)(2,1)S(1)} %copy.16.queries_ref, bf16[1024,128]{1,0:T(8,128)(2,1)S(1)} %copy-done.3, bf16[8,16,2560]{2,1,0:T(8,128)(2,1)S(1)} %bitcast.9, ...), custom_call_target="tpu_custom_call" | custom-call | flops 20000000000 | bytes 20000000 | tf_op jit(solution)/shard_map/attention/pallas_call | solution.py:504
  82.0 0.0 copy-start.4
  82.0 0.0 slice-done
  82.0 0.0 slice-done.1
  82.0 0.0 copy-done.6
  82.0 1.3 fusion.1
  83.3 0.0 copy-done.4
  83.4 0.0 copy-start.5
  83.4 1.3 convolution_convert_fusion
  84.7 0.0 copy-done.5
  84.7 64.4 %experts.1 = (bf16[128,2560]{1,0:T(8,128)(2,1)}, bf16[1,64,2560]{2,1,0:T(8,128)(2,1)}, bf16[1,64,2560]{2,1,0:T(8,128)(2,1)}, bf16[1,64,2560]{2,1,0:T(8,128)(2,1)}) custom-call(bf16[8,16,2560]{2,1,0:T(8,128)(2,1)} %bitcast.12, bf16[2,8,16,2560]{3,2,1,0:T(8,128)(2,1)} %copy-done.4, bf16[2,2,4,64,2560]{4,3,2,1,0:T(8,128)(2,1)} %get-tuple-element.9.weights_ref, ...), custom_call_target="tpu_custom_call" | custom-call | flops 5000000000 | bytes 20000000 | tf_op jit(solution)/shard_map/experts/pallas_call | solution.py:798
  149.1 0.0 copy-start.9
  149.1 0.0 copy-start.8
  149.1 0.0 copy-start.7
  149.1 2.0 %copy.21 = bf16[128,2560]{1,0:T(8,128)(2,1)} copy(bf16[128,2560]{1,0:T(8,128)(2,1)} %get-tuple-element.16) | data formatting | bytes 1310720
  151.2 0.0 copy-done.9
  151.2 0.7 copy.22
  151.9 0.0 copy-done.8
  151.9 0.7 copy.23
  152.6 0.0 copy-done.7
  152.6 0.7 copy.24
  (4 shorter events, 0.0 us)
Async XLA Ops:
  0.6 6.6 %copy-start = (bf16[128,2560]{1,0:T(8,128)(2,1)S(1)}, bf16[128,2560]{1,0:T(8,128)(2,1)}, u32[]{:S(2)}) copy-start(bf16[128,2560]{1,0:T(8,128)(2,1)} %param.21) | copy-start | bytes 1966084
  3.3 4.3 %copy-start.1 = (bf16[1,64,2560]{2,1,0:T(8,128)(2,1)S(1)}, bf16[1,64,2560]{2,1,0:T(8,128)(2,1)}, u32[]{:S(2)}) copy-start(bf16[1,64,2560]{2,1,0:T(8,128)(2,1)} %gate_ref.1) | copy-start | bytes 983044
  3.3 4.3 %copy-start.2 = (bf16[1,64,2560]{2,1,0:T(8,128)(2,1)S(1)}, bf16[1,64,2560]{2,1,0:T(8,128)(2,1)}, u32[]{:S(2)}) copy-start(bf16[1,64,2560]{2,1,0:T(8,128)(2,1)} %up_ref.1) | copy-start | bytes 983044
  3.4 4.3 %copy-start.3 = (bf16[1024,128]{1,0:T(8,128)(2,1)S(1)}, bf16[1024,128]{1,0:T(8,128)(2,1)}, u32[]{:S(2)}) copy-start(bf16[1024,128]{1,0:T(8,128)(2,1)} %keyvals_ref.1) | copy-start | bytes 786436
  7.7 74.3 %slice-start = ((s8[7864320]{0:T(1024)(128)(4,1)}), s8[4194304]{0:T(1024)(128)(4,1)S(1)}, s32[]{:S(2)}) async-start(s8[7864320]{0:T(1024)(128)(4,1)} %bitcast.10), calls=%async_computation | async-start | bytes 8388608
  7.7 74.3 %slice-start.1 = ((s8[7864320]{0:T(1024)(128)(4,1)}), s8[3670016]{0:T(1024)(128)(4,1)S(1)}, s32[]{:S(2)}) async-start(s8[7864320]{0:T(1024)(128)(4,1)} %bitcast.10), calls=%async_computation.1 | async-start | bytes 7340032
  7.7 74.3 %copy-start.6 = (bf16[128,2560]{1,0:T(8,128)(2,1)S(1)}, bf16[128,2560]{1,0:T(8,128)(2,1)}, u32[]{:S(2)}) copy-start(bf16[128,2560]{1,0:T(8,128)(2,1)} %param.11) | copy-start | bytes 1966084
  82.0 1.4 copy-start.4
  83.4 1.3 copy-start.5
  149.1 2.1 %copy-start.9 = (bf16[1,64,2560]{2,1,0:T(8,128)(2,1)S(1)}, bf16[1,64,2560]{2,1,0:T(8,128)(2,1)}, u32[]{:S(2)}) copy-start(bf16[1,64,2560]{2,1,0:T(8,128)(2,1)} %get-tuple-element.17) | copy-start | bytes 983044
  149.1 2.8 %copy-start.8 = (bf16[1,64,2560]{2,1,0:T(8,128)(2,1)S(1)}, bf16[1,64,2560]{2,1,0:T(8,128)(2,1)}, u32[]{:S(2)}) copy-start(bf16[1,64,2560]{2,1,0:T(8,128)(2,1)} %get-tuple-element.18) | copy-start | bytes 983044
  149.1 3.5 %copy-start.7 = (bf16[1,64,2560]{2,1,0:T(8,128)(2,1)S(1)}, bf16[1,64,2560]{2,1,0:T(8,128)(2,1)}, u32[]{:S(2)}) copy-start(bf16[1,64,2560]{2,1,0:T(8,128)(2,1)} %get-tuple-element.19) | copy-start | bytes 983044

commit v6 on v5

--- a/solution.py
+++ b/solution.py
@@ -81,8 +81,7 @@
 FAR_START = 2
 WEIGHTS_START = 4
 PUSH_START = 9
-WEIGHTS_PASS = 14
-WEIGHTS_LAST = 17
+WEIGHTS_PASS = 17
 
 
 def attention_kernel(
@@ -166,8 +165,8 @@
         turned[half, 0] = jnp.concatenate([flat, empty], axis=0)
         turned[half, 1] = jnp.concatenate([empty, flat], axis=0)
 
-    odd_out[...] = queries_ref[pl.ds(half_rows, half_rows), :].T
-    turn(0, queries_ref[pl.ds(0, half_rows), :].T)
+    odd_out[...] = queries_ref[:, pl.ds(half_rows, half_rows)]
+    turn(0, queries_ref[:, pl.ds(0, half_rows)])
     m_ref[...] = jnp.full_like(m_ref, very_negative)
     acc_ref[...] = jnp.zeros_like(acc_ref)
     pl.semaphore_wait(barrier, len(greeted))
@@ -378,12 +377,6 @@
             weight_below.start()
             weight_core[1].start()
 
-        @pl.when(slot == WEIGHTS_LAST)
-        def _():
-            weight_above.wait_recv()
-            weight_below.wait_recv()
-            weight_core[2].start()
-
         def one_half(half, inner):
             last_half, last_block, scored = inner
             seen = slot - ODD_LAG * half
@@ -452,6 +445,10 @@
     @pl.when(ex >= 4)
     def _():
         even_copies[0].start()
+
+    weight_above.wait_recv()
+    weight_below.wait_recv()
+    weight_core[2].start()
 
     def head_arrival(e):
         return pltpu.make_async_remote_copy(
@@ -492,7 +489,7 @@
 
 
 def attend(queries, keyvals, send_grads, w_gate, w_up):
-    row_count, query_width = queries.shape
+    query_width, row_count = queries.shape
     half_rows = row_count // 2
     heads = query_width // HEAD_DIM
     experts, capacity, width = send_grads.shape
@@ -543,16 +540,18 @@
 
 def expert_kernel(
     rows_ref,
-    cot_in,
+    cot_ref,
     weights_ref,
     own_down_ref,
     hidden_ref,
-    combine_ref,
+    dispatch_ref,
     layer_ref,
     grad_gate_ref,
     grad_up_ref,
     grad_down_ref,
     rows_in,
+    cot_in,
+    weights_in,
     down_in,
     out_buf,
     out_in,
@@ -586,7 +585,10 @@
     def source(dz, de):
         return lax.rem(zl + 2 - dz, 2), lax.rem(ex + experts - de, experts)
 
-    down_in[c, y] = own_down_ref[0]
+    own_down = pltpu.make_async_copy(own_down_ref.at[0], down_in.at[c, y], local_sem.at[0])
+    load_weights = pltpu.make_async_copy(weights_ref, weights_in, local_sem.at[3])
+    load_cot = pltpu.make_async_copy(cot_ref, cot_in, local_sem.at[4])
+    own_down.start()
     barrier = pltpu.get_barrier_semaphore()
     for dz, de in offsets[1:]:
         tz, te = peer(dz, de)
@@ -710,6 +712,7 @@
             device_id_type=MESH,
         )
 
+    own_down.wait()
     owned = down_in.shape[2]
     every, low, high = pl.ds(0, owned), pl.ds(0, owned // 2), pl.ds(owned // 2, owned // 2)
     weight_own = [
@@ -717,6 +720,8 @@
         go(weight_copy(1, every, 0, y_down)),
         go(weight_copy(2, every, 0, core_peer)),
     ]
+    load_weights.start()
+    load_cot.start()
     weight_own[0].wait_recv()
     weight_above = go(weight_copy(3, low, 3, y_up))
     weight_core = [go(weight_copy(5, every, 3, core_peer))]
@@ -728,7 +733,9 @@
     weight_core.append(go(weight_copy(7, every, 2, core_peer)))
     for copy in (weight_own[2], *weight_core):
         copy.wait_recv()
-    gate, up = (weights_ref[n].reshape(-1, width) for n in range(2))
+    load_cot.wait()
+    load_weights.wait()
+    gate, up = (weights_in[n].reshape(-1, width) for n in range(2))
     down = down_in[...].reshape(-1, width)
     output_grads = flat(cot_in)
     hidden_grad = contract_cols(output_grads, down)
@@ -775,33 +782,40 @@
     arrive((own_out, back))
     for start in range(0, width, chunk):
         cols = pl.ds(start, chunk)
-        returned = out_in[:, :, :, cols].reshape(tokens, chunk)
-        layer_ref[:, cols] = (
-            wide(hidden_ref[:, cols])
-            + jnp.dot(combine_ref[...], returned, preferred_element_type=jnp.float32)
-        ).astype(jnp.bfloat16)
+        combined = sum(
+            contract_rows(dispatch_ref[...], out_in[z, :, :, cols].reshape(-1, chunk))
+            for z in range(2)
+        )
+        layer_ref[:, cols] = (wide(hidden_ref[:, cols]) + combined).astype(jnp.bfloat16)
     finish(1, full_gate, grad_gate_ref)
     finish(2, full_up, grad_up_ref)
     for copy in (*rows_copies[1], *back, *started):
         copy.wait_send()
 
 
+def hand_on_kernel(*refs):
+    for source, result in zip(refs[:4], refs[4:]):
+        result[...] = source[...]
+
+
 def expert_layer(send_rows, grad_rows, weights, w_down, hidden_state, dispatch_table):
     experts, capacity, width = send_rows.shape
     owned = weights.shape[3]
     token_count = hidden_state.shape[0]
-    combine = jnp.concatenate([dispatch_table, dispatch_table], axis=0).T
     vmem = pl.BlockSpec(memory_space=pltpu.VMEM)
+    anywhere = pl.BlockSpec(memory_space=pl.ANY)
     bf16 = jnp.bfloat16
     landing = pltpu.VMEM((2, experts, capacity, width), bf16)
     grad_shape = jax.ShapeDtypeStruct((1, owned, width), bf16)
-    return pl.pallas_call(
+    results = pl.pallas_call(
         expert_kernel,
         out_shape=(jax.ShapeDtypeStruct((token_count, width), bf16),) + (grad_shape,) * 3,
-        in_specs=[vmem] * 6,
+        in_specs=[anywhere] * 4 + [vmem] * 2,
         out_specs=(vmem,) * 4,
         scratch_shapes=[
             landing,
+            landing,
+            pltpu.VMEM(weights.shape, bf16),
             pltpu.VMEM((2, 4, owned, width), bf16),
             landing,
             landing,
@@ -818,7 +832,7 @@
             pltpu.SemaphoreType.DMA((3, 5)),
             pltpu.SemaphoreType.DMA((8,)),
             pltpu.SemaphoreType.DMA((8,)),
-            pltpu.SemaphoreType.DMA((3,)),
+            pltpu.SemaphoreType.DMA((5,)),
         ],
         compiler_params=pltpu.CompilerParams(
             collective_id=1, has_side_effects=True, vmem_limit_bytes=56 * 2**20
@@ -827,7 +841,14 @@
             flops=5_000_000_000, bytes_accessed=20_000_000, transcendentals=200_000
         ),
         name="experts",
-    )(send_rows, grad_rows, weights, w_down, hidden_state, combine)
+    )(send_rows, grad_rows, weights, w_down, hidden_state, dispatch_table)
+    return pl.pallas_call(
+        hand_on_kernel,
+        out_shape=[jax.ShapeDtypeStruct(r.shape, r.dtype) for r in results],
+        in_specs=[vmem] * 4,
+        out_specs=[vmem] * 4,
+        name="hand_on",
+    )(*results)
 
 
 def local(
@@ -847,7 +868,7 @@
     model_width = resid.shape[1]
     expert_count = lax.axis_size("exp")
     capacity = token_count // expert_count
-    expert_of = jnp.take(hash_table, token_ids)
+    expert_of = hash_table.at[token_ids].get(mode="promise_in_bounds")
     onehot_slots = (
         expert_of[:, None] == jnp.arange(expert_count, dtype=jnp.int32)[None, :]
     ).astype(jnp.int32)
@@ -866,7 +887,7 @@
         )
 
     token_heads, grad_rows, weights = attend(
-        queries, keyvals, placed(cotangent), w_gate, w_up
+        queries.T, keyvals, placed(cotangent), w_gate, w_up
     )
     projected = contract_rows(token_heads.reshape(-1, token_count), out_proj)
     hidden_state = (resid.astype(jnp.float32) + projected).astype(jnp.bfloat16)

time: 154 us -> 143 us (0.929)
  local copies, waits for them, and re-layouts: 7.44 us -> 2.02 us
  Pallas kernels: 139 us -> 135 us
    pallas_call x1, Pallas kernels: 74.3 us -> 65 us  [attend(): pl.pallas_call(attention_kernel, out_shape=(jax.ShapeDtypeStruct((experts...]
    unnamed x29 -> x20, local copies, waits for them, and re-layouts: 5.48 us -> 0.05 us
    pallas_call x1, Pallas kernels: 64.4 us -> 67.2 us  [expert_layer(): pl.pallas_call(expert_kernel, out_shape=(jax.ShapeDtypeStruct((token_coun...]
    pallas_call x0 -> x1, Pallas kernels: none -> 2.55 us  [expert_layer(): pl.pallas_call(hand_on_kernel, out_shape=[jax.ShapeDtypeStruct(r.shape, r...]
where the time goes in v6:
time: 143 us
  Pallas kernels  135 us (94%)
  matrix products  2.9 us (2%)
  other arithmetic  2.57 us (2%)
  local copies, waits for them, and re-layouts  2.02 us (1%)
    pallas_call x1, Pallas kernels, expert_layer(): pl.pallas_call(expert_kernel, out_shape=(jax.ShapeDtypeStruct((token_coun...  67.2 us
    pallas_call x1, Pallas kernels, attend(): pl.pallas_call(attention_kernel, out_shape=(jax.ShapeDtypeStruct((experts...  65 us

profile of v6, /device:TPU:1, one launch (start us, length us, event | category | flops | bytes accessed | tf_op | source)
XLA Modules:
  0.0 143.0 jit_solution(17731850604180432180)
XLA Ops:
  0.6 0.0 copy-start
  0.6 0.0 copy-start.3
  0.7 0.0 copy-start.2
  0.7 0.0 copy-start.4
  0.7 0.0 copy-start.1
  0.7 0.8 compare_select_fusion
  1.5 2.0 %gather_fusion = s32[128]{0:T(128)S(1)} fusion(s32[128256]{0:T(1024)} %param.17, s32[1024]{0:T(1024)S(1)} %pad_clamp_fusion), kind=kCustom, calls=%fused_computation | custom fusion | bytes 1536 | tf_op jit(solution)/shard_map/gather | solution.py:871
  3.5 0.7 convert_element_type.32
  4.2 0.1 fusion.7
  4.2 0.2 reduce_window_sum.11
  4.4 0.2 select_reduce_fusion
  4.6 0.6 fusion.8.dispatch_ref
  5.2 0.0 copy-done
  5.2 0.3 convolution_convert_fusion.1
  5.6 0.0 slice-start
  5.6 0.0 copy-done.3
  5.6 0.0 copy-done.2
  5.6 0.0 copy-done.4
  5.6 0.0 copy-done.1
  5.6 0.0 slice-start.1
  5.6 0.0 copy-start.7
  5.6 65.0 %attention.1 = (bf16[8,192,128]{2,1,0:T(8,128)(2,1)S(1)}, bf16[2,8,16,2560]{3,2,1,0:T(8,128)(2,1)S(1)}, bf16[2,2,4,64,2560]{4,3,2,1,0:T(8,128)(2,1)}) custom-call(bf16[192,1024]{1,0:T(8,128)(2,1)S(1)} %bitcast.9, bf16[1024,128]{1,0:T(8,128)(2,1)S(1)} %copy-done.4, bf16[8,16,2560]{2,1,0:T(8,128)(2,1)S(1)} %bitcast.8, bf16[1,64,2560]{2,1,0:T(8,128)(2,1)S(1)} %copy-done.2, ...), custom_call_target="tpu_custom_call" | custom-call | flops 20000000000 | bytes 20000000 | tf_op jit(solution)/shard_map/attention/pallas_call | solution.py:501
  70.6 0.0 copy-start.5
  70.6 0.0 slice-done
  70.6 0.0 slice-done.1
  70.7 0.0 copy-done.7
  70.7 1.3 fusion.1
  72.0 0.0 copy-done.5
  72.0 0.0 copy-start.6
  72.0 1.3 convolution_convert_fusion
  73.3 0.0 copy-done.6
  73.3 67.2 %experts.1 = (bf16[128,2560]{1,0:T(8,128)(2,1)}, bf16[1,64,2560]{2,1,0:T(8,128)(2,1)}, bf16[1,64,2560]{2,1,0:T(8,128)(2,1)}, bf16[1,64,2560]{2,1,0:T(8,128)(2,1)}) custom-call(bf16[8,16,2560]{2,1,0:T(8,128)(2,1)} %bitcast.12, bf16[2,8,16,2560]{3,2,1,0:T(8,128)(2,1)} %copy-done.5, bf16[2,2,4,64,2560]{4,3,2,1,0:T(8,128)(2,1)} %get-tuple-element.13.weights_ref, ...), custom_call_target="tpu_custom_call" | custom-call | flops 5000000000 | bytes 20000000 | tf_op jit(solution)/shard_map/experts/pallas_call | solution.py:810
  140.5 2.5 %hand_on.1 = (bf16[128,2560]{1,0:T(8,128)(2,1)}, bf16[1,64,2560]{2,1,0:T(8,128)(2,1)}, bf16[1,64,2560]{2,1,0:T(8,128)(2,1)}, bf16[1,64,2560]{2,1,0:T(8,128)(2,1)}) custom-call(bf16[128,2560]{1,0:T(8,128)(2,1)} %get-tuple-element.14.refs_0_, bf16[1,64,2560]{2,1,0:T(8,128)(2,1)} %get-tuple-element.15.refs_1_, bf16[1,64,2560]{2,1,0:T(8,128)(2,1)} %get-tuple-element.16.refs_2_, ...), custom_call_target="tpu_custom_call" | custom-call | tf_op jit(solution)/shard_map/hand_on/pallas_call | solution.py:845
  (4 shorter events, 0.0 us)
Async XLA Ops:
  0.6 4.6 %copy-start = (bf16[128,2560]{1,0:T(8,128)(2,1)S(1)}, bf16[128,2560]{1,0:T(8,128)(2,1)}, u32[]{:S(2)}) copy-start(bf16[128,2560]{1,0:T(8,128)(2,1)} %param.21) | copy-start | bytes 1966084
  0.6 4.9 %copy-start.3 = (bf16[1,64,2560]{2,1,0:T(8,128)(2,1)S(1)}, bf16[1,64,2560]{2,1,0:T(8,128)(2,1)}, u32[]{:S(2)}) copy-start(bf16[1,64,2560]{2,1,0:T(8,128)(2,1)} %up_ref.1) | copy-start | bytes 983044
  0.7 4.9 %copy-start.2 = (bf16[1,64,2560]{2,1,0:T(8,128)(2,1)S(1)}, bf16[1,64,2560]{2,1,0:T(8,128)(2,1)}, u32[]{:S(2)}) copy-start(bf16[1,64,2560]{2,1,0:T(8,128)(2,1)} %gate_ref.1) | copy-start | bytes 983044
  0.7 4.9 %copy-start.4 = (bf16[1024,128]{1,0:T(8,128)(2,1)S(1)}, bf16[1024,128]{1,0:T(8,128)(2,1)}, u32[]{:S(2)}) copy-start(bf16[1024,128]{1,0:T(8,128)(2,1)} %keyvals_ref.1) | copy-start | bytes 786436
  0.7 4.9 %copy-start.1 = (bf16[1024,192]{0,1:T(8,128)(2,1)S(1)}, bf16[1024,192]{0,1:T(8,128)(2,1)}, u32[]{:S(2)}) copy-start(bf16[1024,192]{0,1:T(8,128)(2,1)} %param.12) | copy-start | bytes 1179652
  5.6 65.1 %slice-start = ((s8[7864320]{0:T(1024)(128)(4,1)}), s8[4194304]{0:T(1024)(128)(4,1)S(1)}, s32[]{:S(2)}) async-start(s8[7864320]{0:T(1024)(128)(4,1)} %bitcast.10), calls=%async_computation | async-start | bytes 8388608
  5.6 65.0 %slice-start.1 = ((s8[7864320]{0:T(1024)(128)(4,1)}), s8[3670016]{0:T(1024)(128)(4,1)S(1)}, s32[]{:S(2)}) async-start(s8[7864320]{0:T(1024)(128)(4,1)} %bitcast.10), calls=%async_computation.1 | async-start | bytes 7340032
  5.6 65.0 %copy-start.7 = (bf16[128,2560]{1,0:T(8,128)(2,1)S(1)}, bf16[128,2560]{1,0:T(8,128)(2,1)}, u32[]{:S(2)}) copy-start(bf16[128,2560]{1,0:T(8,128)(2,1)} %param.11) | copy-start | bytes 1966084
  70.6 1.4 copy-start.5
  72.0 1.3 copy-start.6

commit v7 on v6

--- a/solution.py
+++ b/solution.py
@@ -402,9 +402,8 @@
         0, len(ARRIVALS) + ODD_LAG, visit, (jnp.int32(0), shard, jnp.int32(0))
     )
     stage(1, last_half, last_block, (1, mirror, True))
-    stage(0, 1, mirror)
-
-    for half in range(2):
+
+    def settle(half):
         total = acc_ref[half]
         mixed = total[:HEAD_DIM] / total[HEAD_DIM : HEAD_DIM + 1]
         for head in range(heads):
@@ -435,7 +434,8 @@
     own_heads = pltpu.make_async_copy(
         mixed_ref.at[0, lax.rem(ex, 4)], heads_out.at[ex], local_sem.at[4]
     )
-    for copy in (*odd_copies, *even_copies[1:]):
+    settle(0)
+    for copy in even_copies[1:]:
         copy.start()
 
     @pl.when(ex < 4)
@@ -445,6 +445,11 @@
     @pl.when(ex >= 4)
     def _():
         even_copies[0].start()
+
+    stage(0, 1, mirror)
+    settle(1)
+    for copy in odd_copies:
+        copy.start()
 
     weight_above.wait_recv()
     weight_below.wait_recv()
@@ -868,12 +873,18 @@
     model_width = resid.shape[1]
     expert_count = lax.axis_size("exp")
     capacity = token_count // expert_count
-    expert_of = hash_table.at[token_ids].get(mode="promise_in_bounds")
-    onehot_slots = (
-        expert_of[:, None] == jnp.arange(expert_count, dtype=jnp.int32)[None, :]
-    ).astype(jnp.int32)
-    earlier = jnp.cumsum(onehot_slots, axis=0) - onehot_slots
-    slot_of = jnp.sum(onehot_slots * earlier, axis=1)
+    expert_of = lax.gather(
+        hash_table,
+        token_ids[:, None],
+        lax.GatherDimensionNumbers(
+            offset_dims=(), collapsed_slice_dims=(0,), start_index_map=(0,)
+        ),
+        slice_sizes=(1,),
+        mode=lax.GatherScatterMode.PROMISE_IN_BOUNDS,
+    )
+    order = jnp.arange(token_count, dtype=jnp.int32)
+    same_earlier = (expert_of[:, None] == expert_of[None, :]) & (order[:, None] < order[None, :])
+    slot_of = jnp.sum(same_earlier.astype(jnp.int32), axis=0)
     target = jnp.where(slot_of < capacity, expert_of * capacity + slot_of, -1)
     dispatch_table = (
         jnp.arange(expert_count * capacity, dtype=jnp.int32)[:, None] == target[None, :]

time: 143 us -> 143 us (level)
    pallas_call x1, Pallas kernels: 65 us -> 63 us  [attend(): pl.pallas_call(attention_kernel, out_shape=(jax.ShapeDtypeStruct((experts...]
    pallas_call x1, Pallas kernels: 67.2 us -> 69 us  [expert_layer(): pl.pallas_call(expert_kernel, out_shape=(jax.ShapeDtypeStruct((token_coun...]
where the time goes in v7:
time: 143 us
  Pallas kernels  135 us (94%)
  matrix products  2.9 us (2%)
  other arithmetic  2.23 us (2%)
  local copies, waits for them, and re-layouts  2.02 us (1%)
    pallas_call x1, Pallas kernels, expert_layer(): pl.pallas_call(expert_kernel, out_shape=(jax.ShapeDtypeStruct((token_coun...  69 us
    pallas_call x1, Pallas kernels, attend(): pl.pallas_call(attention_kernel, out_shape=(jax.ShapeDtypeStruct((experts...  63 us

profile of v7, /device:TPU:1, one launch (start us, length us, event | category | flops | bytes accessed | tf_op | source)
XLA Modules:
  0.0 142.6 jit_solution(12622384902609815487)
XLA Ops:
  0.6 0.0 copy-start
  0.6 0.0 copy-start.3
  0.7 0.0 copy-start.2
  0.7 0.0 copy-start.4
  0.7 0.0 copy-start.1
  0.7 0.8 pad_clamp_fusion
  1.5 2.0 %gather_fusion = s32[128]{0:T(128)S(1)} fusion(s32[128256]{0:T(1024)} %param.17, s32[1024]{0:T(1024)S(1)} %pad_clamp_fusion), kind=kCustom, calls=%fused_computation | custom fusion | bytes 1536 | tf_op jit(solution)/shard_map/gather | solution.py:876
  3.4 0.1 convert_reduce_fusion
  3.6 0.7 convert_element_type.32
  4.3 0.6 fusion.7.dispatch_ref
  4.9 0.0 copy-done
  4.9 0.3 convolution_convert_fusion.1
  5.2 0.0 slice-start
  5.2 0.0 copy-done.3
  5.2 0.0 copy-done.2
  5.3 0.0 copy-done.4
  5.3 0.0 copy-done.1
  5.3 0.0 slice-start.1
  5.3 0.0 copy-start.7
  5.3 63.0 %attention.1 = (bf16[8,192,128]{2,1,0:T(8,128)(2,1)S(1)}, bf16[2,8,16,2560]{3,2,1,0:T(8,128)(2,1)S(1)}, bf16[2,2,4,64,2560]{4,3,2,1,0:T(8,128)(2,1)}) custom-call(bf16[192,1024]{1,0:T(8,128)(2,1)S(1)} %bitcast.9, bf16[1024,128]{1,0:T(8,128)(2,1)S(1)} %copy-done.4, bf16[8,16,2560]{2,1,0:T(8,128)(2,1)S(1)} %bitcast.8, bf16[1,64,2560]{2,1,0:T(8,128)(2,1)S(1)} %copy-done.2, ...), custom_call_target="tpu_custom_call" | custom-call | flops 20000000000 | bytes 20000000 | tf_op jit(solution)/shard_map/attention/pallas_call | solution.py:506
  68.3 0.0 copy-start.5
  68.4 0.0 slice-done
  68.4 0.0 slice-done.1
  68.4 0.0 copy-done.7
  68.4 1.3 fusion.1
  69.7 0.0 copy-done.5
  69.7 0.0 copy-start.6
  69.7 1.3 convolution_convert_fusion
  71.0 0.0 copy-done.6
  71.0 69.0 %experts.1 = (bf16[128,2560]{1,0:T(8,128)(2,1)}, bf16[1,64,2560]{2,1,0:T(8,128)(2,1)}, bf16[1,64,2560]{2,1,0:T(8,128)(2,1)}, bf16[1,64,2560]{2,1,0:T(8,128)(2,1)}) custom-call(bf16[8,16,2560]{2,1,0:T(8,128)(2,1)} %bitcast.12, bf16[2,8,16,2560]{3,2,1,0:T(8,128)(2,1)} %copy-done.5, bf16[2,2,4,64,2560]{4,3,2,1,0:T(8,128)(2,1)} %get-tuple-element.13.weights_ref, ...), custom_call_target="tpu_custom_call" | custom-call | flops 5000000000 | bytes 20000000 | tf_op jit(solution)/shard_map/experts/pallas_call | solution.py:815
  140.0 2.5 %hand_on.1 = (bf16[128,2560]{1,0:T(8,128)(2,1)}, bf16[1,64,2560]{2,1,0:T(8,128)(2,1)}, bf16[1,64,2560]{2,1,0:T(8,128)(2,1)}, bf16[1,64,2560]{2,1,0:T(8,128)(2,1)}) custom-call(bf16[128,2560]{1,0:T(8,128)(2,1)} %get-tuple-element.14.refs_0_, bf16[1,64,2560]{2,1,0:T(8,128)(2,1)} %get-tuple-element.15.refs_1_, bf16[1,64,2560]{2,1,0:T(8,128)(2,1)} %get-tuple-element.16.refs_2_, ...), custom_call_target="tpu_custom_call" | custom-call | tf_op jit(solution)/shard_map/hand_on/pallas_call | solution.py:850
  (3 shorter events, 0.0 us)
Async XLA Ops:
  0.6 4.3 %copy-start = (bf16[128,2560]{1,0:T(8,128)(2,1)S(1)}, bf16[128,2560]{1,0:T(8,128)(2,1)}, u32[]{:S(2)}) copy-start(bf16[128,2560]{1,0:T(8,128)(2,1)} %param.21) | copy-start | bytes 1966084
  0.6 4.6 %copy-start.3 = (bf16[1,64,2560]{2,1,0:T(8,128)(2,1)S(1)}, bf16[1,64,2560]{2,1,0:T(8,128)(2,1)}, u32[]{:S(2)}) copy-start(bf16[1,64,2560]{2,1,0:T(8,128)(2,1)} %up_ref.1) | copy-start | bytes 983044
  0.7 4.6 %copy-start.2 = (bf16[1,64,2560]{2,1,0:T(8,128)(2,1)S(1)}, bf16[1,64,2560]{2,1,0:T(8,128)(2,1)}, u32[]{:S(2)}) copy-start(bf16[1,64,2560]{2,1,0:T(8,128)(2,1)} %gate_ref.1) | copy-start | bytes 983044
  0.7 4.6 %copy-start.4 = (bf16[1024,128]{1,0:T(8,128)(2,1)S(1)}, bf16[1024,128]{1,0:T(8,128)(2,1)}, u32[]{:S(2)}) copy-start(bf16[1024,128]{1,0:T(8,128)(2,1)} %keyvals_ref.1) | copy-start | bytes 786436
  0.7 4.6 %copy-start.1 = (bf16[1024,192]{0,1:T(8,128)(2,1)S(1)}, bf16[1024,192]{0,1:T(8,128)(2,1)}, u32[]{:S(2)}) copy-start(bf16[1024,192]{0,1:T(8,128)(2,1)} %param.12) | copy-start | bytes 1179652
  5.2 63.1 %slice-start = ((s8[7864320]{0:T(1024)(128)(4,1)}), s8[4194304]{0:T(1024)(128)(4,1)S(1)}, s32[]{:S(2)}) async-start(s8[7864320]{0:T(1024)(128)(4,1)} %bitcast.10), calls=%async_computation | async-start | bytes 8388608
  5.3 63.1 %slice-start.1 = ((s8[7864320]{0:T(1024)(128)(4,1)}), s8[3670016]{0:T(1024)(128)(4,1)S(1)}, s32[]{:S(2)}) async-start(s8[7864320]{0:T(1024)(128)(4,1)} %bitcast.10), calls=%async_computation.1 | async-start | bytes 7340032
  5.3 63.1 %copy-start.7 = (bf16[128,2560]{1,0:T(8,128)(2,1)S(1)}, bf16[128,2560]{1,0:T(8,128)(2,1)}, u32[]{:S(2)}) copy-start(bf16[128,2560]{1,0:T(8,128)(2,1)} %param.11) | copy-start | bytes 1966084
  68.3 1.4 copy-start.5
  69.7 1.3 copy-start.6
